TPU v7x, 32 devices: a whole 2x2x4 slice. The times are simulated.
32 devices in a mesh: groups: 2 (over x), tile: 16 (over z, y, core).
Axes of the slice: x: 2, y: 2, z: 4, core: 2. Of those that a mesh axis runs over, the one named last changes fastest.
Arguments:
- start_model: float32 [2, 32768, 128], P(None, ('groups', 'tile')), parts along dimension 1, may hold values from -6 to 6
- v_basis: bfloat16 [2, 26624, 1024], P(None, ('groups', 'tile')), parts along dimension 1, may hold values from -0.125 to 0.125
- u_basis: bfloat16 [2, 1, 832, 32768], P(None, None, None, ('groups', 'tile')), parts along dimension 3, may hold values from -0.15625 to 0.15625
- records: bfloat16 [32, 128, 32768], P(None, None, ('groups', 'tile')), parts along dimension 2, may hold values from -6 to 6
- tile_ranks: int32 [2, 16, 16], P('groups'), parts along dimension 0, may hold values from 8 to 96, as said below
- window_start: int32 [128, 32768], P(None, ('groups', 'tile')), parts along dimension 1, may hold values from 0 to 7, as said below
- window_stop: int32 [128, 32768], P(None, ('groups', 'tile')), parts along dimension 1, may hold values from 16 to 31
Outputs:
- final_model: float32 [2, 32768, 128], P(None, ('groups', 'tile')), parts along dimension 1
There are 2 independent parts, one for each index of `groups`. A program takes and returns all parts, laid end to end along the dimension named above; each array names one. Nothing has to cross between parts.
Inputs may be any that keep to these rules, and one draw needn't show every extreme that they name: `tile_ranks`: every tile row and every tile column of one frequency holds the same 16 ranks, each once, and they sum to 832; every frequency has tiles of rank 96 and of rank 8. window_stop - window_start lies between 16 and 24 for every pair.
All inputs are finite; a program needn't handle non-finite values.
Results may differ from a plain program's by a relative error of at most 0.012.
Values may be sent and summed in bfloat16 or wider, within the bound.
No kernel may reach another device: no remote copies, remote signals or barrier semaphores. Data moves between devices by JAX's collectives and lax.ppermute only.
A program may use at most 128 MiB of HBM per device.

v0:
```python
import functools
import math

import jax
import jax.numpy as jnp
import numpy as np
from jax import lax
from jax.experimental import pallas as pl
from jax.experimental.pallas import tpu as pltpu
from jax.sharding import PartitionSpec as P

RMAX = 96
ITERS = 2
STEP = 0.5
START_MAX = 7
STOP_MIN = 16
STOP_MAX = 31
F32 = jnp.float32
BF16 = jnp.bfloat16

SMEM = pl.BlockSpec(memory_space=pltpu.SMEM)
VMEM = pl.BlockSpec(memory_space=pltpu.VMEM)
PARAMS = pltpu.CompilerParams(vmem_limit_bytes=12 * 1024 * 1024)


def phase_rows(freq_count, sample_count):
    moments = np.arange(sample_count, dtype=np.float64)
    bins = np.arange(freq_count, dtype=np.float64) + 1.0
    phases = 2.0 * math.pi / sample_count * bins[:, None] * moments[None, :]
    factor = math.sqrt(2.0 / sample_count)
    rows = np.stack([np.cos(phases), -np.sin(phases)], axis=1) * factor
    return rows.reshape(2 * freq_count, sample_count).astype(np.float32)


def pair_list(count):
    return [(a, b) for a in range(count) for b in range(a, count)]


def side_by_side(real, imag):
    return jnp.concatenate([real, imag], axis=1).astype(BF16)


def dot(left, right):
    return jnp.dot(left, right, preferred_element_type=F32)


def dot_last(left, right):
    return lax.dot_general(left, right, (((1,), (1,)), ((), ())), preferred_element_type=F32)


def above(upper, lower):
    return jnp.concatenate([upper, lower], axis=0).astype(BF16)


def rows_turned(rows_ref, rank_total):
    return rows_ref[0, :rank_total, :].T, rows_ref[1, :rank_total, :].T


def store_slots(ranks_of, rows_ref, slots_ref, slot_count, repeat, first_slot):
    start = 0
    for k in range(slot_count):
        block = jnp.concatenate([rows_ref[c, pl.ds(start, RMAX), :] for c in range(2)], axis=1)
        block = block.astype(BF16)
        for p in range(repeat):
            slots_ref[first_slot + k * repeat + p] = block
        start = start + ranks_of(k)


def piece_tree(blocks):
    while len(blocks) > 1:
        half = len(blocks) // 2
        blocks = [
            (blocks[q].astype(F32) + blocks[q + half].astype(F32)).astype(BF16)
            for q in range(half)
        ]
    return blocks[0]


def load_slots(ranks_of, slots_ref, rows_ref, slot_count, repeat, first_slot):
    start = 0
    lanes = rows_ref.shape[2]
    for k in range(slot_count):
        block = piece_tree([slots_ref[first_slot + k * repeat + p] for p in range(repeat)])
        block = block.astype(F32)
        for c in range(2):
            rows_ref[c, pl.ds(start, RMAX), :] = block[:, c * lanes : (c + 1) * lanes]
        start = start + ranks_of(k)


def clear_tail(rows_ref, rank_total):
    tail = (2, rows_ref.shape[1] - rank_total, rows_ref.shape[2])
    rows_ref[:, rank_total:, :] = jnp.zeros(tail, F32)


def store_rows(rows_ref, rank_total, value):
    lanes = rows_ref.shape[2]
    for c in range(2):
        rows_ref[c, :rank_total, :] = value[:, c * lanes : (c + 1) * lanes]


def column_of(ranks_ref):
    cols = ranks_ref.shape[2]
    device = lax.axis_index("tile")
    freq, col = device // cols, device % cols
    return lambda i: ranks_ref[freq, i, col]


def project(v_ref, real, imag, rows_ref):
    rank_total = v_ref.shape[1]
    value = dot(v_ref[0], side_by_side(real, imag)) + dot(v_ref[1], side_by_side(-imag, real))
    store_rows(rows_ref, rank_total, value)


def first_kernel(pieces, ranks_ref, v_ref, x_ref, slots_ref, rows_ref):
    clear_tail(rows_ref, v_ref.shape[1])
    project(v_ref, x_ref[0], x_ref[1], rows_ref)
    store_slots(column_of(ranks_ref), rows_ref, slots_ref, ranks_ref.shape[1], pieces, 0)


def misfit_kernel(
    pieces, ranks_ref, in_ref, u_ref, gram_ref, data_ref, out_ref, rows_ref, pred_ref, field_ref
):
    freqs, _, cols = ranks_ref.shape
    rank_total, width = u_ref.shape[2:]
    lanes = in_ref.shape[2] // 2
    row = lax.axis_index("tile") // pieces
    for f in range(freqs):
        ranks_of = lambda j, f=f: ranks_ref[f, row, j]
        load_slots(ranks_of, in_ref, rows_ref, cols, 1, f * cols)
        real, imag = rows_turned(rows_ref, rank_total)
        pred_ref[f] = dot(above(real, imag), u_ref[0, f]) + dot(above(-imag, real), u_ref[1, f])
    parts = 2 * freqs
    where = {pair: k for k, pair in enumerate(pair_list(parts))}
    clear_tail(rows_ref, rank_total)
    for a in range(parts):
        total = -data_ref[a]
        for b in range(parts):
            half = pred_ref[b // 2, b % 2 * lanes : (b % 2 + 1) * lanes, :]
            total = total + gram_ref[where[(min(a, b), max(a, b))]] * half
        field_ref[a] = total.astype(BF16)
    for f in range(freqs):
        ranks_of = lambda j, f=f: ranks_ref[f, row, j]
        real, imag = field_ref[2 * f], field_ref[2 * f + 1]
        value = dot_last(u_ref[0, f], above(real, imag)) + dot_last(
            u_ref[1, f], above(imag, -real)
        )
        store_rows(rows_ref, rank_total, value)
        store_slots(ranks_of, rows_ref, out_ref, cols, 1, f * cols)


def update_kernel(pieces, last, ranks_ref, in_ref, v_ref, x_ref, *rest):
    if last:
        new_ref, rows_ref = rest
    else:
        new_ref, slots_ref, rows_ref = rest
    rank_total = v_ref.shape[1]
    lanes = in_ref.shape[2] // 2
    ranks_of = column_of(ranks_ref)
    load_slots(ranks_of, in_ref, rows_ref, ranks_ref.shape[1], pieces, 0)
    real, imag = rows_turned(rows_ref, rank_total)
    gradient = dot(above(real, imag), v_ref[0]) + dot(above(imag, -real), v_ref[1])
    new_ref[0] = x_ref[0] - STEP * gradient[:lanes].T
    new_ref[1] = x_ref[1] - STEP * gradient[lanes:].T
    if not last:
        clear_tail(rows_ref, rank_total)
        project(v_ref, new_ref[0], new_ref[1], rows_ref)
        store_slots(ranks_of, rows_ref, slots_ref, ranks_ref.shape[1], pieces, 0)


def harmonic_sums(freq_count, sample_count):
    multiples = np.arange(2 * freq_count + 1, dtype=np.float64)[:, None]
    phases = 2.0 * math.pi / sample_count * multiples * np.arange(sample_count)[None, :]
    waves = np.stack([np.cos(phases), np.sin(phases)]) / sample_count
    sums = np.concatenate([np.zeros((2, waves.shape[1], 1)), np.cumsum(waves, axis=2)], axis=2)
    return sums.astype(np.float32)


def gram_parts(a, b):
    f, g = a // 2 + 1, b // 2 + 1
    apart, lean = abs(f - g), 1.0 if f > g else -1.0 if f < g else 0.0
    if a % 2 == 0 and b % 2 == 0:
        return [(0, apart, 1.0), (0, f + g, 1.0)]
    if a % 2 == 1 and b % 2 == 1:
        return [(0, apart, 1.0), (0, f + g, -1.0)]
    if a % 2 == 0:
        return [(1, apart, lean), (1, f + g, -1.0)]
    return [(1, apart, -lean), (1, f + g, -1.0)]


def normal_kernel(phases, start_ref, stop_ref, records_ref, gram_ref, data_ref):
    parts, samples = phases.shape
    half = samples // 2
    pairs = pair_list(parts)
    sums = harmonic_sums(parts // 2, samples)
    terms = [[term for term in gram_parts(a, b) if term[2] != 0.0] for a, b in pairs]
    needed = sorted({(kind, k) for some in terms for kind, k, _ in some if (kind, k) != (1, 0)})
    chunk = 16

    def pick(level, table, first, last):
        value = jnp.full(level.shape, float(table[first]), F32)
        for t in range(first + 1, last + 1):
            value = jnp.where(level >= t, float(table[t]), value)
        return value

    def add_up(step, carry):
        rows = pl.ds(pl.multiple_of(step * chunk, chunk), chunk)
        begin, end = start_ref[rows, :], stop_ref[rows, :]
        waves = {}
        for kind, k in needed:
            if (kind, k) == (0, 0):
                waves[kind, k] = (end - begin).astype(F32) * (1.0 / samples)
            else:
                table = sums[kind, k]
                waves[kind, k] = pick(end, table, STOP_MIN, STOP_MAX) - pick(
                    begin, table, 0, START_MAX
                )
        for n, some in enumerate(terms):
            total = None
            for kind, k, sign in some:
                if (kind, k) == (1, 0):
                    continue
                if total is None:
                    total = waves[kind, k] if sign > 0 else -waves[kind, k]
                else:
                    total = total + waves[kind, k] if sign > 0 else total - waves[kind, k]
            gram_ref[n, rows, :] = total

        def seen(t):
            value = records_ref[t, rows, :].astype(F32)
            if t < START_MAX:
                value = jnp.where(begin <= t, value, 0.0)
            if t >= STOP_MIN:
                value = jnp.where(end > t, value, 0.0)
            return value

        for odd in (0, 1):
            some = [a for a in range(parts) if (a // 2 + 1) % 2 == odd]
            datas = [jnp.zeros(begin.shape, F32) for _ in some]
            for t in range(half if some else 0):
                late, early = t + half, seen(t)
                if late < STOP_MAX:
                    early = early - seen(late) if odd else early + seen(late)
                for k, a in enumerate(some):
                    datas[k] = datas[k] + float(phases[a, t]) * early
            for k, a in enumerate(some):
                data_ref[a, rows, :] = datas[k]
        return carry

    lax.fori_loop(0, start_ref.shape[0] // chunk, add_up, 0)


def normal_terms(phases, window_start, window_stop, records):
    samples, lanes, width = records.shape
    parts = phases.shape[0]
    pair_count = len(pair_list(parts))
    block = 128
    return pl.pallas_call(
        functools.partial(normal_kernel, phases),
        grid=(width // block,),
        in_specs=[
            pl.BlockSpec((lanes, block), lambda n: (0, n)),
            pl.BlockSpec((lanes, block), lambda n: (0, n)),
            pl.BlockSpec((samples, lanes, block), lambda n: (0, 0, n)),
        ],
        out_specs=[
            pl.BlockSpec((pair_count, lanes, block), lambda n: (0, 0, n)),
            pl.BlockSpec((parts, lanes, block), lambda n: (0, 0, n)),
        ],
        out_shape=[
            jax.ShapeDtypeStruct((pair_count, lanes, width), F32),
            jax.ShapeDtypeStruct((parts, lanes, width), F32),
        ],
        cost_estimate=pl.CostEstimate(
            flops=16 * records.size, bytes_accessed=3 * records.size, transcendentals=0
        ),
        compiler_params=PARAMS,
        name="normal_terms",
    )(window_start, window_stop, records)


def on_device(start_model, v_basis, u_basis, records, tile_ranks, window_start, window_stop):
    tiles = lax.axis_size("tile")
    freqs, rows, cols = tile_ranks.shape
    pieces = tiles // rows
    rank_total = v_basis.shape[1]
    lanes = start_model.shape[2]
    receivers = u_basis.shape[3]
    phases = phase_rows(freqs, records.shape[0])

    slots = jax.ShapeDtypeStruct((tiles, RMAX, 2 * lanes), BF16)
    model = jax.ShapeDtypeStruct(start_model.shape, F32)
    padded_rows = pltpu.VMEM((2, rank_total + RMAX, lanes), F32)
    exchange = lambda x: lax.all_to_all(x, "tile", split_axis=0, concat_axis=0, tiled=True)

    outgoing = pl.pallas_call(
        functools.partial(first_kernel, pieces),
        in_specs=[SMEM, VMEM, VMEM],
        out_specs=VMEM,
        out_shape=slots,
        scratch_shapes=[padded_rows],
        compiler_params=PARAMS,
        name="first_projection",
    )(tile_ranks, v_basis, start_model)
    gram, data = normal_terms(phases, window_start, window_stop, records)
    current = start_model
    for iteration in range(ITERS):
        arrived = exchange(outgoing)
        outgoing = pl.pallas_call(
            functools.partial(misfit_kernel, pieces),
            in_specs=[SMEM] + [VMEM] * 4,
            out_specs=VMEM,
            out_shape=slots,
            scratch_shapes=[
                padded_rows,
                pltpu.VMEM((freqs, 2 * lanes, receivers), F32),
                pltpu.VMEM((2 * freqs, lanes, receivers), BF16),
            ],
            compiler_params=PARAMS,
            name="misfit",
        )(tile_ranks, arrived, u_basis, gram, data)
        arrived = exchange(outgoing)
        last = iteration == ITERS - 1
        result = pl.pallas_call(
            functools.partial(update_kernel, pieces, last),
            in_specs=[SMEM] + [VMEM] * 3,
            out_specs=VMEM if last else [VMEM, VMEM],
            out_shape=model if last else [model, slots],
            scratch_shapes=[padded_rows],
            compiler_params=PARAMS,
            name="last_update" if last else "update",
        )(tile_ranks, arrived, v_basis, current)
        if last:
            current = result
        else:
            current, outgoing = result
    return current


def solution(mesh):
    in_specs = (
        P(None, ("groups", "tile"), None),
        P(None, ("groups", "tile"), None),
        P(None, None, None, ("groups", "tile")),
        P(None, None, ("groups", "tile")),
        P("groups", None, None),
        P(None, ("groups", "tile")),
        P(None, ("groups", "tile")),
    )
    out_specs = P(None, ("groups", "tile"), None)
    return jax.shard_map(
        on_device, mesh=mesh, in_specs=in_specs, out_specs=out_specs, check_vma=False
    )
```

profile of v0, /device:TPU:1, one launch (start us, length us, event | category | flops | bytes accessed | tf_op | source)
XLA Modules:
  0.0 122.7 jit_solution(460250293016920737)
XLA Ops:
  0.0 2.0 %copy-done = bf16[2,832,1024]{2,1,0:T(8,128)(2,1)S(1)} copy-done((bf16[2,832,1024]{2,1,0:T(8,128)(2,1)S(1)}, bf16[2,832,1024]{2,1,0:T(8,128)(2,1)}, u32[]{:S(2)}) %copy-start) | copy-done | bytes 3407896
  2.0 1.2 copy-done.6
  3.2 0.7 copy-done.12
  3.9 2.7 %first_projection.1 = bf16[16,96,256]{2,1,0:T(8,128)(2,1)} custom-call(s32[1,16,16]{2,1,0:T(8,128)S(1)} %copy-done.12, bf16[2,832,1024]{2,1,0:T(8,128)(2,1)S(1)} %copy-done, f32[2,1024,128]{2,1,0:T(8,128)S(1)} %copy-done.6), custom_call_target="tpu_custom_call" | custom-call | tf_op jit(solution)/shard_map/first_projection/pallas_call | solution.py:295
  6.6 7.3 %all-to-all-start = ((bf16[16,96,256]{2,1,0:T(8,128)(2,1)}), bf16[16,96,256]{2,1,0:T(8,128)(2,1)}, u32[]{:S(2)}, u32[]{:S(2)}) async-start(bf16[16,96,256]{2,1,0:T(8,128)(2,1)} %first_projection.1), calls=%async_computation | async-start | bytes 1572864 | tf_op jit(solution)/shard_map/all_to_all | solution.py:293
  13.9 3.4 %copy-done.3 = bf16[32,128,1024]{2,1,0:T(8,128)(2,1)S(1)} copy-done((bf16[32,128,1024]{2,1,0:T(8,128)(2,1)S(1)}, bf16[32,128,1024]{2,1,0:T(8,128)(2,1)}, u32[]{:S(2)}) %copy-start.3) | copy-done | bytes 8388632
  17.3 1.0 copy-done.10
  18.4 1.0 copy-done.11
  19.4 7.5 %normal_terms.1 = (f32[3,128,1024]{2,1,0:T(8,128)S(1)}, f32[2,128,1024]{2,1,0:T(8,128)S(1)}) custom-call(s32[128,1024]{1,0:T(8,128)S(1)} %copy-done.10, s32[128,1024]{1,0:T(8,128)S(1)} %copy-done.11, bf16[32,128,1024]{2,1,0:T(8,128)(2,1)S(1)} %copy-done.3), custom_call_target="tpu_custom_call" | custom-call | flops 67108864 | bytes 12582912 | tf_op jit(solution)/shard_map/normal_terms/pallas_call | solution.py:257
  26.9 0.0 copy-start.4
  27.0 1.2 copy-done.4
  28.1 1.0 copy-done.8
  29.1 3.5 %all-to-all-done.in_ref = bf16[16,96,256]{2,1,0:T(8,128)(2,1)} async-done(((bf16[16,96,256]{2,1,0:T(8,128)(2,1)}), bf16[16,96,256]{2,1,0:T(8,128)(2,1)}, u32[]{:S(2)}, u32[]{:S(2)}) %all-to-all-start) | async-done | bytes 786464 | tf_op jit(solution)/shard_map/all_to_all | solution.py:293
  32.6 0.0 copy-done.2
  32.6 0.0 copy-done.13
  32.6 1.4 %copy-done.5 = f32[3,128,1024]{2,1,0:T(8,128)S(1)} copy-done((f32[3,128,1024]{2,1,0:T(8,128)S(1)}, f32[3,128,1024]{2,1,0:T(8,128)}, u32[]{:S(2)}) %copy-start.5) | copy-done | bytes 1572888
  34.0 1.2 copy-done.9
  35.2 3.9 %misfit.2 = bf16[16,96,256]{2,1,0:T(8,128)(2,1)S(1)} custom-call(s32[1,16,16]{2,1,0:T(8,128)S(1)} %copy-done.13, bf16[16,96,256]{2,1,0:T(8,128)(2,1)} %all-to-all-done.in_ref, bf16[2,1,832,1024]{3,2,1,0:T(8,128)(2,1)S(1)} %copy-done.2, f32[3,128,1024]{2,1,0:T(8,128)S(1)} %copy-done.5, f32[2,128,1024]{2,1,0:T(8,128)S(1)} %copy-done.9), custom_call_target="tpu_custom_call" | custom-call | tf_op jit(solution)/shard_map/misfit/pallas_call | solution.py:308
  39.1 26.1 %all_to_all.20.in_ref = bf16[16,96,256]{2,1,0:T(8,128)(2,1)S(1)} all-to-all(bf16[16,96,256]{2,1,0:T(8,128)(2,1)S(1)} %misfit.2), channel_id=1, replica_groups=mesh['groups'=2,'tile'=16] {'tile'}, dimensions={0} | all-to-all | bytes 1572864 | tf_op jit(solution)/shard_map/all_to_all | solution.py:293
  65.2 3.1 %update.1 = (f32[2,1024,128]{2,1,0:T(8,128)S(1)}, bf16[16,96,256]{2,1,0:T(8,128)(2,1)S(1)}) custom-call(s32[1,16,16]{2,1,0:T(8,128)S(1)} %copy-done.13, bf16[16,96,256]{2,1,0:T(8,128)(2,1)S(1)} %all_to_all.20.in_ref, bf16[2,832,1024]{2,1,0:T(8,128)(2,1)S(1)} %copy-done.1, f32[2,1024,128]{2,1,0:T(8,128)S(1)} %copy-done.7), custom_call_target="tpu_custom_call" | custom-call | tf_op jit(solution)/shard_map/update/pallas_call | solution.py:323
  68.2 24.0 %all_to_all.21.in_ref = bf16[16,96,256]{2,1,0:T(8,128)(2,1)S(1)} all-to-all(bf16[16,96,256]{2,1,0:T(8,128)(2,1)S(1)} %get-tuple-element.11), channel_id=1, replica_groups=mesh['groups'=2,'tile'=16] {'tile'}, dimensions={0} | all-to-all | bytes 1572864 | tf_op jit(solution)/shard_map/all_to_all | solution.py:293
  92.2 3.2 %misfit.3 = bf16[16,96,256]{2,1,0:T(8,128)(2,1)S(1)} custom-call(s32[1,16,16]{2,1,0:T(8,128)S(1)} %copy-done.13, bf16[16,96,256]{2,1,0:T(8,128)(2,1)S(1)} %all_to_all.21.in_ref, bf16[2,1,832,1024]{3,2,1,0:T(8,128)(2,1)S(1)} %copy-done.2, f32[3,128,1024]{2,1,0:T(8,128)S(1)} %copy-done.5, f32[2,128,1024]{2,1,0:T(8,128)S(1)} %copy-done.9), custom_call_target="tpu_custom_call" | custom-call | tf_op jit(solution)/shard_map/misfit/pallas_call | solution.py:308
  95.5 24.0 %all_to_all.22.in_ref = bf16[16,96,256]{2,1,0:T(8,128)(2,1)S(1)} all-to-all(bf16[16,96,256]{2,1,0:T(8,128)(2,1)S(1)} %misfit.3), channel_id=1, replica_groups=mesh['groups'=2,'tile'=16] {'tile'}, dimensions={0} | all-to-all | bytes 1572864 | tf_op jit(solution)/shard_map/all_to_all | solution.py:293
  119.5 3.2 %last_update.1 = f32[2,1024,128]{2,1,0:T(8,128)} custom-call(s32[1,16,16]{2,1,0:T(8,128)S(1)} %copy-done.13, bf16[16,96,256]{2,1,0:T(8,128)(2,1)S(1)} %all_to_all.22.in_ref, bf16[2,832,1024]{2,1,0:T(8,128)(2,1)S(1)} %copy-done.1, f32[2,1024,128]{2,1,0:T(8,128)S(1)} %get-tuple-element.12.x_ref), custom_call_target="tpu_custom_call" | custom-call | tf_op jit(solution)/shard_map/last_update/pallas_call | solution.py:323
  (15 shorter events, 0.0 us)
Async XLA Ops:
  0.0 2.0 %copy-start = (bf16[2,832,1024]{2,1,0:T(8,128)(2,1)S(1)}, bf16[2,832,1024]{2,1,0:T(8,128)(2,1)}, u32[]{:S(2)}) copy-start(bf16[2,832,1024]{2,1,0:T(8,128)(2,1)} %v_ref.5) | copy-start | bytes 10223620
  2.0 1.2 copy-start.6
  3.2 0.7 copy-start.12
  6.6 26.0 %all-to-all-start = ((bf16[16,96,256]{2,1,0:T(8,128)(2,1)}), bf16[16,96,256]{2,1,0:T(8,128)(2,1)}, u32[]{:S(2)}, u32[]{:S(2)}) async-start(bf16[16,96,256]{2,1,0:T(8,128)(2,1)} %first_projection.1), calls=%async_computation | async-start | bytes 1572864 | tf_op jit(solution)/shard_map/all_to_all | solution.py:293
  13.9 3.4 %copy-start.3 = (bf16[32,128,1024]{2,1,0:T(8,128)(2,1)S(1)}, bf16[32,128,1024]{2,1,0:T(8,128)(2,1)}, u32[]{:S(2)}) copy-start(bf16[32,128,1024]{2,1,0:T(8,128)(2,1)} %records_ref.1) | copy-start | bytes 25165828
  17.3 1.0 copy-start.10
  18.4 1.0 copy-start.11
  19.4 13.2 %copy-start.2 = (bf16[2,1,832,1024]{3,2,1,0:T(8,128)(2,1)S(1)}, bf16[2,1,832,1024]{3,2,1,0:T(8,128)(2,1)}, u32[]{:S(2)}) copy-start(bf16[2,1,832,1024]{3,2,1,0:T(8,128)(2,1)} %u_ref.3) | copy-start | bytes 10223620
  19.4 13.2 %copy-start.13 = (s32[1,16,16]{2,1,0:T(8,128)S(1)}, s32[1,16,16]{2,1,0:T(8,128)}, u32[]{:S(2)}) copy-start(s32[1,16,16]{2,1,0:T(8,128)} %ranks_ref.9) | copy-start | bytes 3076
  26.9 1.2 copy-start.4
  28.1 1.0 copy-start.8
  32.6 1.4 %copy-start.5 = (f32[3,128,1024]{2,1,0:T(8,128)S(1)}, f32[3,128,1024]{2,1,0:T(8,128)}, u32[]{:S(2)}) copy-start(f32[3,128,1024]{2,1,0:T(8,128)} %copy-done.4) | copy-start | bytes 4718596
  34.0 1.2 copy-start.9
  35.2 29.9 %copy-start.1 = (bf16[2,832,1024]{2,1,0:T(8,128)(2,1)S(1)}, bf16[2,832,1024]{2,1,0:T(8,128)(2,1)}, u32[]{:S(2)}) copy-start(bf16[2,832,1024]{2,1,0:T(8,128)(2,1)} %v_ref.5) | copy-start | bytes 10223620
  35.2 29.9 %copy-start.7 = (f32[2,1024,128]{2,1,0:T(8,128)S(1)}, f32[2,1024,128]{2,1,0:T(8,128)}, u32[]{:S(2)}) copy-start(f32[2,1024,128]{2,1,0:T(8,128)} %x_ref.3) | copy-start | bytes 3145732
where the time goes:
time: 123 us
  blocking collectives  74 us (60%)
  Pallas kernels  23.6 us (19%)
  local copies, waits for them, and re-layouts  14.1 us (11%)
  starting transfers between devices  7.35 us (6%)
  waiting for transfers between devices  3.5 us (3%)
    all_to_all x3, blocking collectives, on_device(): lax.all_to_all(x, 'tile', split_axis=0, concat_axis=0, tiled=True)  74 us
    unnamed x28, local copies, waits for them, and re-layouts  14.1 us
    pallas_call x1, Pallas kernels, normal_terms(): pl.pallas_call(functools.partial(normal_kernel, phases), grid=(width // b...  7.54 us
    all_to_all x1, starting transfers between devices, on_device(): lax.all_to_all(x, 'tile', split_axis=0, concat_axis=0, tiled=True)  7.35 us
    pallas_call x2, Pallas kernels, on_device(): pl.pallas_call(functools.partial(misfit_kernel, pieces), in_specs=[SMEM]...  7.11 us
    pallas_call x2, Pallas kernels, on_device(): pl.pallas_call(functools.partial(update_kernel, pieces, last), in_specs=[...  6.28 us
    all_to_all x1, waiting for transfers between devices, on_device(): lax.all_to_all(x, 'tile', split_axis=0, concat_axis=0, tiled=True)  3.5 us
    pallas_call x1, Pallas kernels, on_device(): pl.pallas_call(functools.partial(first_kernel, pieces), in_specs=[SMEM, V...  2.69 us
  transfers between devices with their start and end apart: 1, of which 1 were waited for; matrix products, arithmetic and copies ran while one was open for 0% of the time, Pallas kernels for 6%

commit v1 on v0

--- a/solution.py
+++ b/solution.py
@@ -20,7 +20,16 @@
 
 SMEM = pl.BlockSpec(memory_space=pltpu.SMEM)
 VMEM = pl.BlockSpec(memory_space=pltpu.VMEM)
-PARAMS = pltpu.CompilerParams(vmem_limit_bytes=12 * 1024 * 1024)
+HBM = pl.BlockSpec(memory_space=pltpu.HBM)
+MIB = 1024 * 1024
+
+
+def mebibytes(*arrays):
+    return sum(-(-x.size * x.dtype.itemsize // MIB) for x in arrays)
+
+
+def params(mib):
+    return pltpu.CompilerParams(vmem_limit_bytes=mib * MIB)
 
 
 def phase_rows(freq_count, sample_count):
@@ -52,17 +61,15 @@
     return jnp.concatenate([upper, lower], axis=0).astype(BF16)
 
 
-def rows_turned(rows_ref, rank_total):
-    return rows_ref[0, :rank_total, :].T, rows_ref[1, :rank_total, :].T
-
-
-def store_slots(ranks_of, rows_ref, slots_ref, slot_count, repeat, first_slot):
+def store_slots(ranks_of, rows_ref, slots_ref, slot_count, repeat, first_slot, done=None):
     start = 0
     for k in range(slot_count):
         block = jnp.concatenate([rows_ref[c, pl.ds(start, RMAX), :] for c in range(2)], axis=1)
         block = block.astype(BF16)
         for p in range(repeat):
             slots_ref[first_slot + k * repeat + p] = block
+            if done is not None:
+                done(first_slot + k * repeat + p)
         start = start + ranks_of(k)
 
 
@@ -105,65 +112,162 @@
     return lambda i: ranks_ref[freq, i, col]
 
 
-def project(v_ref, real, imag, rows_ref):
-    rank_total = v_ref.shape[1]
-    value = dot(v_ref[0], side_by_side(real, imag)) + dot(v_ref[1], side_by_side(-imag, real))
-    store_rows(rows_ref, rank_total, value)
-
-
-def first_kernel(pieces, ranks_ref, v_ref, x_ref, slots_ref, rows_ref):
+def turned_stack(real, imag):
+    return jnp.concatenate([side_by_side(*real), side_by_side(*imag)], axis=0).T
+
+
+def chunks(width):
+    size = math.gcd(width, 256)
+    return [pl.ds(k, size) for k in range(0, width, size)]
+
+
+def flat(block):
+    return block.reshape(block.shape[0] * block.shape[1], block.shape[2])
+
+
+def project(v_ref, waves_ref, rows_ref):
+    value = dot(v_ref[0], waves_ref[0]) + dot(v_ref[1], waves_ref[1])
+    store_rows(rows_ref, v_ref.shape[1], value)
+
+
+def first_kernel(
+    pieces,
+    ranks_hbm,
+    v_hbm,
+    x_hbm,
+    slots_hbm,
+    ranks_ref,
+    v_ref,
+    x_ref,
+    waves_ref,
+    rows_ref,
+    slots_ref,
+    in_sems,
+    out_sems,
+):
+    pairs = [(x_hbm, x_ref), (v_hbm, v_ref), (ranks_hbm, ranks_ref)]
+    copies = [pltpu.make_async_copy(*pair, in_sems.at[n]) for n, pair in enumerate(pairs)]
+    for copy in copies:
+        copy.start()
     clear_tail(rows_ref, v_ref.shape[1])
-    project(v_ref, x_ref[0], x_ref[1], rows_ref)
-    store_slots(column_of(ranks_ref), rows_ref, slots_ref, ranks_ref.shape[1], pieces, 0)
+    copies[0].wait()
+    real, imag = x_ref[0], x_ref[1]
+    waves_ref[0] = side_by_side(real, imag)
+    waves_ref[1] = side_by_side(-imag, real)
+    copies[1].wait()
+    copies[2].wait()
+    project(v_ref, waves_ref, rows_ref)
+    sent = []
+
+    def send(last_slot):
+        group = slots_ref.shape[0] // out_sems.shape[0]
+        if last_slot % group == group - 1:
+            these = pl.ds(last_slot - group + 1, group)
+            sem = out_sems.at[last_slot // group]
+            sent.append(pltpu.make_async_copy(slots_ref.at[these], slots_hbm.at[these], sem))
+            sent[-1].start()
+
+    ranks_of = column_of(ranks_ref)
+    store_slots(ranks_of, rows_ref, slots_ref, ranks_ref.shape[1], pieces, 0, send)
+    for copy in sent:
+        copy.wait()
 
 
 def misfit_kernel(
-    pieces, ranks_ref, in_ref, u_ref, gram_ref, data_ref, out_ref, rows_ref, pred_ref, field_ref
+    pieces,
+    cold,
+    ranks_ref,
+    in_ref,
+    u_ref,
+    gram_ref,
+    data_ref,
+    *rest,
 ):
     freqs, _, cols = ranks_ref.shape
     rank_total, width = u_ref.shape[2:]
+    if cold:
+        slots_hbm, gram_hbm, data_hbm = in_ref, gram_ref, data_ref
+        out_ref, rows_ref, left_ref, field_ref, *fetch = rest
+        in_ref, gram_ref, data_ref, pred_ref, sems = fetch
+        pairs = [(slots_hbm, in_ref), (gram_hbm, gram_ref), (data_hbm, data_ref)]
+        copies = [pltpu.make_async_copy(*pair, sems.at[n]) for n, pair in enumerate(pairs)]
+        for copy in copies:
+            copy.start()
+        copies[0].wait()
+    else:
+        out_ref, rows_ref, left_ref, field_ref = rest
     lanes = in_ref.shape[2] // 2
     row = lax.axis_index("tile") // pieces
     for f in range(freqs):
         ranks_of = lambda j, f=f: ranks_ref[f, row, j]
         load_slots(ranks_of, in_ref, rows_ref, cols, 1, f * cols)
-        real, imag = rows_turned(rows_ref, rank_total)
-        pred_ref[f] = dot(above(real, imag), u_ref[0, f]) + dot(above(-imag, real), u_ref[1, f])
+        real, imag = rows_ref[0, :rank_total, :], rows_ref[1, :rank_total, :]
+        left_ref[f] = turned_stack((real, imag), (-imag, real))
     parts = 2 * freqs
     where = {pair: k for k, pair in enumerate(pair_list(parts))}
     clear_tail(rows_ref, rank_total)
-    for a in range(parts):
-        total = -data_ref[a]
-        for b in range(parts):
-            half = pred_ref[b // 2, b % 2 * lanes : (b % 2 + 1) * lanes, :]
-            total = total + gram_ref[where[(min(a, b), max(a, b))]] * half
-        field_ref[a] = total.astype(BF16)
+    if cold:
+        for f in range(freqs):
+            pred_ref[f] = dot(left_ref[f], flat(u_ref[:, f]))
+        copies[1].wait()
+        copies[2].wait()
+    for some in chunks(width):
+        preds = []
+        for f in range(freqs):
+            if cold:
+                pred = pred_ref[f, :, some]
+            else:
+                pred = dot(left_ref[f], flat(u_ref[:, f, :, some]))
+            preds += [pred[:lanes], pred[lanes:]]
+        fields = []
+        for a in range(parts):
+            total = -data_ref[a, :, some]
+            for b in range(parts):
+                total = total + gram_ref[where[min(a, b), max(a, b)], :, some] * preds[b]
+            fields.append(total)
+        for f in range(freqs):
+            real, imag = fields[2 * f], fields[2 * f + 1]
+            field_ref[f, 0, :, some] = above(real, imag)
+            field_ref[f, 1, :, some] = above(imag, -real)
     for f in range(freqs):
         ranks_of = lambda j, f=f: ranks_ref[f, row, j]
-        real, imag = field_ref[2 * f], field_ref[2 * f + 1]
-        value = dot_last(u_ref[0, f], above(real, imag)) + dot_last(
-            u_ref[1, f], above(imag, -real)
-        )
+        value = dot_last(u_ref[0, f], field_ref[f, 0]) + dot_last(u_ref[1, f], field_ref[f, 1])
         store_rows(rows_ref, rank_total, value)
         store_slots(ranks_of, rows_ref, out_ref, cols, 1, f * cols)
 
 
 def update_kernel(pieces, last, ranks_ref, in_ref, v_ref, x_ref, *rest):
     if last:
-        new_ref, rows_ref = rest
+        new_hbm, rows_ref, left_ref, new_ref, sems = rest
     else:
-        new_ref, slots_ref, rows_ref = rest
-    rank_total = v_ref.shape[1]
+        new_ref, slots_ref, rows_ref, left_ref, waves_ref = rest
+    rank_total, points = v_ref.shape[1:]
     lanes = in_ref.shape[2] // 2
     ranks_of = column_of(ranks_ref)
     load_slots(ranks_of, in_ref, rows_ref, ranks_ref.shape[1], pieces, 0)
-    real, imag = rows_turned(rows_ref, rank_total)
-    gradient = dot(above(real, imag), v_ref[0]) + dot(above(imag, -real), v_ref[1])
-    new_ref[0] = x_ref[0] - STEP * gradient[:lanes].T
-    new_ref[1] = x_ref[1] - STEP * gradient[lanes:].T
-    if not last:
+    real, imag = rows_ref[0, :rank_total, :], rows_ref[1, :rank_total, :]
+    left_ref[...] = turned_stack((real, imag), (imag, -real))
+    copies = []
+    for k, some in enumerate(chunks(points)):
+        gradient = dot(left_ref[...], flat(v_ref[:, :, some]))
+        real = x_ref[0, some, :] - STEP * gradient[:lanes].T
+        imag = x_ref[1, some, :] - STEP * gradient[lanes:].T
+        new_ref[0, some, :] = real
+        new_ref[1, some, :] = imag
+        if last:
+            copies.append(
+                pltpu.make_async_copy(new_ref.at[:, some, :], new_hbm.at[:, some, :], sems.at[k])
+            )
+            copies[k].start()
+        else:
+            waves_ref[0, some, :] = side_by_side(real, imag)
+            waves_ref[1, some, :] = side_by_side(-imag, real)
+    if last:
+        for copy in copies:
+            copy.wait()
+    else:
         clear_tail(rows_ref, rank_total)
-        project(v_ref, new_ref[0], new_ref[1], rows_ref)
+        project(v_ref, waves_ref, rows_ref)
         store_slots(ranks_of, rows_ref, slots_ref, ranks_ref.shape[1], pieces, 0)
 
 
@@ -273,7 +377,7 @@
         cost_estimate=pl.CostEstimate(
             flops=16 * records.size, bytes_accessed=3 * records.size, transcendentals=0
         ),
-        compiler_params=PARAMS,
+        compiler_params=params(60),
         name="normal_terms",
     )(window_start, window_stop, records)
 
@@ -283,50 +387,75 @@
     freqs, rows, cols = tile_ranks.shape
     pieces = tiles // rows
     rank_total = v_basis.shape[1]
-    lanes = start_model.shape[2]
+    points, lanes = start_model.shape[1:]
     receivers = u_basis.shape[3]
     phases = phase_rows(freqs, records.shape[0])
 
     slots = jax.ShapeDtypeStruct((tiles, RMAX, 2 * lanes), BF16)
     model = jax.ShapeDtypeStruct(start_model.shape, F32)
     padded_rows = pltpu.VMEM((2, rank_total + RMAX, lanes), F32)
+    waves = pltpu.VMEM((2, points, 2 * lanes), BF16)
+    left = pltpu.VMEM((2 * lanes, 2 * rank_total), BF16)
     exchange = lambda x: lax.all_to_all(x, "tile", split_axis=0, concat_axis=0, tiled=True)
 
     outgoing = pl.pallas_call(
         functools.partial(first_kernel, pieces),
-        in_specs=[SMEM, VMEM, VMEM],
-        out_specs=VMEM,
+        in_specs=[HBM, HBM, HBM],
+        out_specs=HBM,
         out_shape=slots,
-        scratch_shapes=[padded_rows],
-        compiler_params=PARAMS,
+        scratch_shapes=[
+            pltpu.SMEM(tile_ranks.shape, tile_ranks.dtype),
+            pltpu.VMEM(v_basis.shape, BF16),
+            pltpu.VMEM(start_model.shape, F32),
+            waves,
+            padded_rows,
+            pltpu.VMEM(slots.shape, BF16),
+            pltpu.SemaphoreType.DMA((3,)),
+            pltpu.SemaphoreType.DMA((2,)),
+        ],
+        compiler_params=params(60),
         name="first_projection",
     )(tile_ranks, v_basis, start_model)
-    gram, data = normal_terms(phases, window_start, window_stop, records)
+    normal = normal_terms(phases, window_start, window_stop, records)
+    in_hbm = lambda x: pltpu.with_memory_space_constraint(x, pltpu.HBM)
+    fetch = [
+        pltpu.VMEM(slots.shape, BF16),
+        *[pltpu.VMEM(x.shape, F32) for x in normal],
+        pltpu.VMEM((freqs, 2 * lanes, receivers), F32),
+        pltpu.SemaphoreType.DMA((3,)),
+    ]
+    finish = [
+        pltpu.VMEM(start_model.shape, F32),
+        pltpu.SemaphoreType.DMA((len(chunks(points)),)),
+    ]
     current = start_model
     for iteration in range(ITERS):
+        cold = iteration == 0
+        terms = [in_hbm(x) for x in normal] if cold else normal
         arrived = exchange(outgoing)
         outgoing = pl.pallas_call(
-            functools.partial(misfit_kernel, pieces),
-            in_specs=[SMEM] + [VMEM] * 4,
+            functools.partial(misfit_kernel, pieces, cold),
+            in_specs=[SMEM, HBM, VMEM, HBM, HBM] if cold else [SMEM] + [VMEM] * 4,
             out_specs=VMEM,
             out_shape=slots,
             scratch_shapes=[
                 padded_rows,
-                pltpu.VMEM((freqs, 2 * lanes, receivers), F32),
-                pltpu.VMEM((2 * freqs, lanes, receivers), BF16),
-            ],
-            compiler_params=PARAMS,
+                pltpu.VMEM((freqs, 2 * lanes, 2 * rank_total), BF16),
+                pltpu.VMEM((freqs, 2, 2 * lanes, receivers), BF16),
+            ]
+            + (fetch if cold else []),
+            compiler_params=params(8 + mebibytes(slots, *normal)),
             name="misfit",
-        )(tile_ranks, arrived, u_basis, gram, data)
+        )(tile_ranks, arrived, u_basis, *terms)
         arrived = exchange(outgoing)
         last = iteration == ITERS - 1
         result = pl.pallas_call(
             functools.partial(update_kernel, pieces, last),
             in_specs=[SMEM] + [VMEM] * 3,
-            out_specs=VMEM if last else [VMEM, VMEM],
+            out_specs=HBM if last else [VMEM, VMEM],
             out_shape=model if last else [model, slots],
-            scratch_shapes=[padded_rows],
-            compiler_params=PARAMS,
+            scratch_shapes=[padded_rows, left] + (finish if last else [waves]),
+            compiler_params=params(12),
             name="last_update" if last else "update",
         )(tile_ranks, arrived, v_basis, current)
         if last:

time: 123 us -> 118 us (0.959)
  local copies, waits for them, and re-layouts: 14.1 us -> 0.02 us
  waiting for transfers between devices: 3.5 us -> 8.96 us
  Pallas kernels: 23.6 us -> 27.6 us
    unnamed x28 -> x12, local copies, waits for them, and re-layouts: 14.1 us -> 0.02 us
    all_to_all x1, waiting for transfers between devices: 3.5 us -> 8.96 us  [on_device(): lax.all_to_all(x, 'tile', split_axis=0, concat_axis=0, tiled=True)]
    pallas_call x3, Pallas kernels: 9.8 us -> 12.1 us  [the longest x2 7.8 us: on_device(): pl.pallas_call(functools.partial(misfit_kernel, pieces, cold), in_specs=[...]
    pallas_call x1, Pallas kernels: 7.54 us -> 9.68 us  [normal_terms(): pl.pallas_call(functools.partial(normal_kernel, phases), grid=(width // b...]
  transfers between devices with their start and end apart: 1 -> 1, of which waited for: 1 -> 1; matrix products, arithmetic and copies ran while one was open for 0% -> 0% of each run, Pallas kernels for 6% -> 8%
where the time goes in v1:
time: 118 us
  blocking collectives  74 us (63%)
  Pallas kernels  27.6 us (23%)
  waiting for transfers between devices  8.96 us (8%)
  starting transfers between devices  7.36 us (6%)
    all_to_all x3, blocking collectives, on_device(): lax.all_to_all(x, 'tile', split_axis=0, concat_axis=0, tiled=True)  74 us
    pallas_call x1, Pallas kernels, normal_terms(): pl.pallas_call(functools.partial(normal_kernel, phases), grid=(width // b...  9.68 us
    all_to_all x1, waiting for transfers between devices, on_device(): lax.all_to_all(x, 'tile', split_axis=0, concat_axis=0, tiled=True)  8.96 us
    pallas_call x2, Pallas kernels, on_device(): pl.pallas_call(functools.partial(misfit_kernel, pieces, cold), in_specs=[...  7.8 us
    all_to_all x1, starting transfers between devices, on_device(): lax.all_to_all(x, 'tile', split_axis=0, concat_axis=0, tiled=True)  7.36 us
    pallas_call x2, Pallas kernels, on_device(): pl.pallas_call(functools.partial(update_kernel, pieces, last), in_specs=[...  5.8 us
    pallas_call x1, Pallas kernels, on_device(): pl.pallas_call(functools.partial(first_kernel, pieces), in_specs=[HBM, HB...  4.31 us
  transfers between devices with their start and end apart: 1, of which 1 were waited for; matrix products, arithmetic and copies ran while one was open for 0% of the time, Pallas kernels for 8%

profile of v1, /device:TPU:1, one launch (start us, length us, event | category | flops | bytes accessed | tf_op | source)
XLA Modules:
  0.0 118.0 jit_solution(16062955278443280394)
XLA Ops:
  0.0 4.3 %first_projection.1 = bf16[16,96,256]{2,1,0:T(8,128)(2,1)} custom-call(s32[1,16,16]{2,1,0:T(8,128)} %ranks_ref.7, bf16[2,832,1024]{2,1,0:T(8,128)(2,1)} %v_ref.3, f32[2,1024,128]{2,1,0:T(8,128)} %x_ref.1), custom_call_target="tpu_custom_call" | custom-call | tf_op jit(solution)/shard_map/first_projection/pallas_call | solution.py:401
  4.3 7.4 %all-to-all-start = ((bf16[16,96,256]{2,1,0:T(8,128)(2,1)}), bf16[16,96,256]{2,1,0:T(8,128)(2,1)}, u32[]{:S(2)}, u32[]{:S(2)}) async-start(bf16[16,96,256]{2,1,0:T(8,128)(2,1)} %first_projection.1), calls=%async_computation | async-start | bytes 1572864 | tf_op jit(solution)/shard_map/all_to_all | solution.py:399
  11.7 0.0 copy-start.1
  11.7 0.0 copy-start.5
  11.7 9.7 %normal_terms.1 = (f32[3,128,1024]{2,1,0:T(8,128)}, f32[2,128,1024]{2,1,0:T(8,128)}) custom-call(s32[128,1024]{1,0:T(8,128)} %start_ref.1, s32[128,1024]{1,0:T(8,128)} %stop_ref.1, bf16[32,128,1024]{2,1,0:T(8,128)(2,1)} %records_ref.1), custom_call_target="tpu_custom_call" | custom-call | flops 67108864 | bytes 12582912 | tf_op jit(solution)/shard_map/normal_terms/pallas_call | solution.py:361
  21.4 9.0 %all-to-all-done.in_ref = bf16[16,96,256]{2,1,0:T(8,128)(2,1)} async-done(((bf16[16,96,256]{2,1,0:T(8,128)(2,1)}), bf16[16,96,256]{2,1,0:T(8,128)(2,1)}, u32[]{:S(2)}, u32[]{:S(2)}) %all-to-all-start) | async-done | bytes 786464 | tf_op jit(solution)/shard_map/all_to_all | solution.py:399
  30.3 0.0 copy-done.1
  30.3 0.0 copy-done.5
  30.3 0.0 copy-start
  30.3 0.0 copy-start.3
  30.4 4.7 %misfit.2 = bf16[16,96,256]{2,1,0:T(8,128)(2,1)S(1)} custom-call(s32[1,16,16]{2,1,0:T(8,128)S(1)} %copy-done.5, bf16[16,96,256]{2,1,0:T(8,128)(2,1)} %all-to-all-done.in_ref, bf16[2,1,832,1024]{3,2,1,0:T(8,128)(2,1)S(1)} %copy-done.1, f32[3,128,1024]{2,1,0:T(8,128)} %get-tuple-element.9.gram_ref, f32[2,128,1024]{2,1,0:T(8,128)} %get-tuple-element.10.data_ref), custom_call_target="tpu_custom_call" | custom-call | tf_op jit(solution)/shard_map/misfit/pallas_call | solution.py:436
  35.0 26.1 %all_to_all.20.in_ref = bf16[16,96,256]{2,1,0:T(8,128)(2,1)S(1)} all-to-all(bf16[16,96,256]{2,1,0:T(8,128)(2,1)S(1)} %misfit.2), channel_id=1, replica_groups=mesh['groups'=2,'tile'=16] {'tile'}, dimensions={0} | all-to-all | bytes 1572864 | tf_op jit(solution)/shard_map/all_to_all | solution.py:399
  61.1 0.0 copy-done
  61.1 0.0 copy-done.3
  61.1 0.0 copy-start.2
  61.1 0.0 copy-start.4
  61.1 2.9 %update.1 = (f32[2,1024,128]{2,1,0:T(8,128)S(1)}, bf16[16,96,256]{2,1,0:T(8,128)(2,1)S(1)}) custom-call(s32[1,16,16]{2,1,0:T(8,128)S(1)} %copy-done.5, bf16[16,96,256]{2,1,0:T(8,128)(2,1)S(1)} %all_to_all.20.in_ref, bf16[2,832,1024]{2,1,0:T(8,128)(2,1)S(1)} %copy-done, f32[2,1024,128]{2,1,0:T(8,128)S(1)} %copy-done.3), custom_call_target="tpu_custom_call" | custom-call | tf_op jit(solution)/shard_map/update/pallas_call | solution.py:452
  64.0 24.0 %all_to_all.21.in_ref = bf16[16,96,256]{2,1,0:T(8,128)(2,1)S(1)} all-to-all(bf16[16,96,256]{2,1,0:T(8,128)(2,1)S(1)} %get-tuple-element.11), channel_id=1, replica_groups=mesh['groups'=2,'tile'=16] {'tile'}, dimensions={0} | all-to-all | bytes 1572864 | tf_op jit(solution)/shard_map/all_to_all | solution.py:399
  88.0 0.0 copy-done.2
  88.0 0.0 copy-done.4
  88.0 3.1 %misfit.3 = bf16[16,96,256]{2,1,0:T(8,128)(2,1)S(1)} custom-call(s32[1,16,16]{2,1,0:T(8,128)S(1)} %copy-done.5, bf16[16,96,256]{2,1,0:T(8,128)(2,1)S(1)} %all_to_all.21.in_ref, bf16[2,1,832,1024]{3,2,1,0:T(8,128)(2,1)S(1)} %copy-done.1, f32[3,128,1024]{2,1,0:T(8,128)S(1)} %copy-done.2, f32[2,128,1024]{2,1,0:T(8,128)S(1)} %copy-done.4), custom_call_target="tpu_custom_call" | custom-call | tf_op jit(solution)/shard_map/misfit/pallas_call | solution.py:436
  91.2 24.0 %all_to_all.22.in_ref = bf16[16,96,256]{2,1,0:T(8,128)(2,1)S(1)} all-to-all(bf16[16,96,256]{2,1,0:T(8,128)(2,1)S(1)} %misfit.3), channel_id=1, replica_groups=mesh['groups'=2,'tile'=16] {'tile'}, dimensions={0} | all-to-all | bytes 1572864 | tf_op jit(solution)/shard_map/all_to_all | solution.py:399
  115.1 2.9 %last_update.1 = f32[2,1024,128]{2,1,0:T(8,128)} custom-call(s32[1,16,16]{2,1,0:T(8,128)S(1)} %copy-done.5, bf16[16,96,256]{2,1,0:T(8,128)(2,1)S(1)} %all_to_all.22.in_ref, bf16[2,832,1024]{2,1,0:T(8,128)(2,1)S(1)} %copy-done, f32[2,1024,128]{2,1,0:T(8,128)S(1)} %get-tuple-element.12.x_ref), custom_call_target="tpu_custom_call" | custom-call | tf_op jit(solution)/shard_map/last_update/pallas_call | solution.py:452
Async XLA Ops:
  4.3 26.0 %all-to-all-start = ((bf16[16,96,256]{2,1,0:T(8,128)(2,1)}), bf16[16,96,256]{2,1,0:T(8,128)(2,1)}, u32[]{:S(2)}, u32[]{:S(2)}) async-start(bf16[16,96,256]{2,1,0:T(8,128)(2,1)} %first_projection.1), calls=%async_computation | async-start | bytes 1572864 | tf_op jit(solution)/shard_map/all_to_all | solution.py:399
  11.7 18.7 %copy-start.1 = (bf16[2,1,832,1024]{3,2,1,0:T(8,128)(2,1)S(1)}, bf16[2,1,832,1024]{3,2,1,0:T(8,128)(2,1)}, u32[]{:S(2)}) copy-start(bf16[2,1,832,1024]{3,2,1,0:T(8,128)(2,1)} %u_ref.3) | copy-start | bytes 10223620
  11.7 18.7 %copy-start.5 = (s32[1,16,16]{2,1,0:T(8,128)S(1)}, s32[1,16,16]{2,1,0:T(8,128)}, u32[]{:S(2)}) copy-start(s32[1,16,16]{2,1,0:T(8,128)} %ranks_ref.7) | copy-start | bytes 3076
  30.3 30.8 %copy-start = (bf16[2,832,1024]{2,1,0:T(8,128)(2,1)S(1)}, bf16[2,832,1024]{2,1,0:T(8,128)(2,1)}, u32[]{:S(2)}) copy-start(bf16[2,832,1024]{2,1,0:T(8,128)(2,1)} %v_ref.3) | copy-start | bytes 10223620
  30.3 30.8 %copy-start.3 = (f32[2,1024,128]{2,1,0:T(8,128)S(1)}, f32[2,1024,128]{2,1,0:T(8,128)}, u32[]{:S(2)}) copy-start(f32[2,1024,128]{2,1,0:T(8,128)} %x_ref.1) | copy-start | bytes 3145732
  61.1 26.9 %copy-start.2 = (f32[3,128,1024]{2,1,0:T(8,128)S(1)}, f32[3,128,1024]{2,1,0:T(8,128)}, u32[]{:S(2)}) copy-start(f32[3,128,1024]{2,1,0:T(8,128)} %get-tuple-element.9.gram_ref) | copy-start | bytes 4718596
  61.1 26.9 %copy-start.4 = (f32[2,128,1024]{2,1,0:T(8,128)S(1)}, f32[2,128,1024]{2,1,0:T(8,128)}, u32[]{:S(2)}) copy-start(f32[2,128,1024]{2,1,0:T(8,128)} %get-tuple-element.10.data_ref) | copy-start | bytes 3145732

commit v2 on v1

--- a/solution.py
+++ b/solution.py
@@ -61,16 +61,34 @@
     return jnp.concatenate([upper, lower], axis=0).astype(BF16)
 
 
-def store_slots(ranks_of, rows_ref, slots_ref, slot_count, repeat, first_slot, done=None):
-    start = 0
-    for k in range(slot_count):
+def running(ranks):
+    starts = [0]
+    for rank in ranks[:-1]:
+        starts.append(starts[-1] + rank)
+    return starts
+
+
+def row_starts(ranks_ref, pieces):
+    freqs, _, cols = ranks_ref.shape
+    row = lax.axis_index("tile") // pieces
+    return [running([ranks_ref[f, row, j] for j in range(cols)]) for f in range(freqs)]
+
+
+def column_starts(ranks_ref):
+    _, rows, cols = ranks_ref.shape
+    device = lax.axis_index("tile")
+    freq, col = device // cols, device % cols
+    return running([ranks_ref[freq, i, col] for i in range(rows)])
+
+
+def store_slots(starts, rows_ref, slots_ref, repeat, first_slot, done=None):
+    for k, start in enumerate(starts):
         block = jnp.concatenate([rows_ref[c, pl.ds(start, RMAX), :] for c in range(2)], axis=1)
         block = block.astype(BF16)
         for p in range(repeat):
             slots_ref[first_slot + k * repeat + p] = block
             if done is not None:
                 done(first_slot + k * repeat + p)
-        start = start + ranks_of(k)
 
 
 def piece_tree(blocks):
@@ -83,15 +101,13 @@
     return blocks[0]
 
 
-def load_slots(ranks_of, slots_ref, rows_ref, slot_count, repeat, first_slot):
-    start = 0
+def load_slots(starts, slots_ref, rows_ref, repeat, first_slot):
     lanes = rows_ref.shape[2]
-    for k in range(slot_count):
+    for k, start in enumerate(starts):
         block = piece_tree([slots_ref[first_slot + k * repeat + p] for p in range(repeat)])
         block = block.astype(F32)
         for c in range(2):
             rows_ref[c, pl.ds(start, RMAX), :] = block[:, c * lanes : (c + 1) * lanes]
-        start = start + ranks_of(k)
 
 
 def clear_tail(rows_ref, rank_total):
@@ -103,13 +119,6 @@
     lanes = rows_ref.shape[2]
     for c in range(2):
         rows_ref[c, :rank_total, :] = value[:, c * lanes : (c + 1) * lanes]
-
-
-def column_of(ranks_ref):
-    cols = ranks_ref.shape[2]
-    device = lax.axis_index("tile")
-    freq, col = device // cols, device % cols
-    return lambda i: ranks_ref[freq, i, col]
 
 
 def turned_stack(real, imag):
@@ -145,17 +154,17 @@
     in_sems,
     out_sems,
 ):
-    pairs = [(x_hbm, x_ref), (v_hbm, v_ref), (ranks_hbm, ranks_ref)]
+    pairs = [(ranks_hbm, ranks_ref), (x_hbm, x_ref), (v_hbm, v_ref)]
     copies = [pltpu.make_async_copy(*pair, in_sems.at[n]) for n, pair in enumerate(pairs)]
     for copy in copies:
         copy.start()
     clear_tail(rows_ref, v_ref.shape[1])
-    copies[0].wait()
+    copies[1].wait()
     real, imag = x_ref[0], x_ref[1]
     waves_ref[0] = side_by_side(real, imag)
     waves_ref[1] = side_by_side(-imag, real)
-    copies[1].wait()
     copies[2].wait()
+    copies[0].wait()
     project(v_ref, waves_ref, rows_ref)
     sent = []
 
@@ -167,8 +176,7 @@
             sent.append(pltpu.make_async_copy(slots_ref.at[these], slots_hbm.at[these], sem))
             sent[-1].start()
 
-    ranks_of = column_of(ranks_ref)
-    store_slots(ranks_of, rows_ref, slots_ref, ranks_ref.shape[1], pieces, 0, send)
+    store_slots(column_starts(ranks_ref), rows_ref, slots_ref, pieces, 0, send)
     for copy in sent:
         copy.wait()
 
@@ -176,31 +184,38 @@
 def misfit_kernel(
     pieces,
     cold,
-    ranks_ref,
+    starts_ref,
     in_ref,
     u_ref,
     gram_ref,
     data_ref,
     *rest,
 ):
-    freqs, _, cols = ranks_ref.shape
-    rank_total, width = u_ref.shape[2:]
+    freqs, rank_total, width = u_ref.shape[1:]
+    cols = in_ref.shape[0] // freqs
     if cold:
         slots_hbm, gram_hbm, data_hbm = in_ref, gram_ref, data_ref
         out_ref, rows_ref, left_ref, field_ref, *fetch = rest
-        in_ref, gram_ref, data_ref, pred_ref, sems = fetch
-        pairs = [(slots_hbm, in_ref), (gram_hbm, gram_ref), (data_hbm, data_ref)]
+        ranks_hbm = starts_ref
+        ranks_ref, in_ref, gram_ref, data_ref, pred_ref, sems = fetch
+        pairs = [
+            (ranks_hbm, ranks_ref),
+            (slots_hbm, in_ref),
+            (gram_hbm, gram_ref),
+            (data_hbm, data_ref),
+        ]
         copies = [pltpu.make_async_copy(*pair, sems.at[n]) for n, pair in enumerate(pairs)]
         for copy in copies:
             copy.start()
         copies[0].wait()
+        copies[1].wait()
+        starts = row_starts(ranks_ref, pieces)
     else:
         out_ref, rows_ref, left_ref, field_ref = rest
+        starts = [[starts_ref[f * cols + j, 0] for j in range(cols)] for f in range(freqs)]
     lanes = in_ref.shape[2] // 2
-    row = lax.axis_index("tile") // pieces
     for f in range(freqs):
-        ranks_of = lambda j, f=f: ranks_ref[f, row, j]
-        load_slots(ranks_of, in_ref, rows_ref, cols, 1, f * cols)
+        load_slots(starts[f], in_ref, rows_ref, 1, f * cols)
         real, imag = rows_ref[0, :rank_total, :], rows_ref[1, :rank_total, :]
         left_ref[f] = turned_stack((real, imag), (-imag, real))
     parts = 2 * freqs
@@ -209,8 +224,8 @@
     if cold:
         for f in range(freqs):
             pred_ref[f] = dot(left_ref[f], flat(u_ref[:, f]))
-        copies[1].wait()
         copies[2].wait()
+        copies[3].wait()
     for some in chunks(width):
         preds = []
         for f in range(freqs):
@@ -230,21 +245,21 @@
             field_ref[f, 0, :, some] = above(real, imag)
             field_ref[f, 1, :, some] = above(imag, -real)
     for f in range(freqs):
-        ranks_of = lambda j, f=f: ranks_ref[f, row, j]
         value = dot_last(u_ref[0, f], field_ref[f, 0]) + dot_last(u_ref[1, f], field_ref[f, 1])
         store_rows(rows_ref, rank_total, value)
-        store_slots(ranks_of, rows_ref, out_ref, cols, 1, f * cols)
-
-
-def update_kernel(pieces, last, ranks_ref, in_ref, v_ref, x_ref, *rest):
+        store_slots(starts[f], rows_ref, out_ref, 1, f * cols)
+
+
+def update_kernel(pieces, last, starts_ref, in_ref, v_ref, x_ref, *rest):
     if last:
         new_hbm, rows_ref, left_ref, new_ref, sems = rest
     else:
         new_ref, slots_ref, rows_ref, left_ref, waves_ref = rest
     rank_total, points = v_ref.shape[1:]
     lanes = in_ref.shape[2] // 2
-    ranks_of = column_of(ranks_ref)
-    load_slots(ranks_of, in_ref, rows_ref, ranks_ref.shape[1], pieces, 0)
+    tiles = in_ref.shape[0]
+    starts = [starts_ref[tiles + i, 0] for i in range(tiles // pieces)]
+    load_slots(starts, in_ref, rows_ref, pieces, 0)
     real, imag = rows_ref[0, :rank_total, :], rows_ref[1, :rank_total, :]
     left_ref[...] = turned_stack((real, imag), (imag, -real))
     copies = []
@@ -268,7 +283,7 @@
     else:
         clear_tail(rows_ref, rank_total)
         project(v_ref, waves_ref, rows_ref)
-        store_slots(ranks_of, rows_ref, slots_ref, ranks_ref.shape[1], pieces, 0)
+        store_slots(starts, rows_ref, slots_ref, pieces, 0)
 
 
 def harmonic_sums(freq_count, sample_count):
@@ -291,7 +306,15 @@
     return [(1, apart, -lean), (1, f + g, -1.0)]
 
 
-def normal_kernel(phases, start_ref, stop_ref, records_ref, gram_ref, data_ref):
+def normal_kernel(
+    phases, pieces, ranks_ref, start_ref, stop_ref, records_ref, gram_ref, data_ref, starts_ref
+):
+    @pl.when(pl.program_id(0) == 0)
+    def _():
+        starts = sum(row_starts(ranks_ref, pieces), []) + column_starts(ranks_ref)
+        for k, start in enumerate(starts):
+            starts_ref[k, :] = jnp.full(starts_ref.shape[1:], start, jnp.int32)
+
     parts, samples = phases.shape
     half = samples // 2
     pairs = pair_list(parts)
@@ -353,15 +376,18 @@
     lax.fori_loop(0, start_ref.shape[0] // chunk, add_up, 0)
 
 
-def normal_terms(phases, window_start, window_stop, records):
+def normal_terms(phases, pieces, tile_ranks, window_start, window_stop, records):
     samples, lanes, width = records.shape
     parts = phases.shape[0]
     pair_count = len(pair_list(parts))
     block = 128
+    freqs, rows, cols = tile_ranks.shape
+    starts = (freqs * cols + rows, block)
     return pl.pallas_call(
-        functools.partial(normal_kernel, phases),
+        functools.partial(normal_kernel, phases, pieces),
         grid=(width // block,),
         in_specs=[
+            SMEM,
             pl.BlockSpec((lanes, block), lambda n: (0, n)),
             pl.BlockSpec((lanes, block), lambda n: (0, n)),
             pl.BlockSpec((samples, lanes, block), lambda n: (0, 0, n)),
@@ -369,17 +395,19 @@
         out_specs=[
             pl.BlockSpec((pair_count, lanes, block), lambda n: (0, 0, n)),
             pl.BlockSpec((parts, lanes, block), lambda n: (0, 0, n)),
+            pl.BlockSpec(starts, lambda n: (0, 0)),
         ],
         out_shape=[
             jax.ShapeDtypeStruct((pair_count, lanes, width), F32),
             jax.ShapeDtypeStruct((parts, lanes, width), F32),
+            jax.ShapeDtypeStruct(starts, jnp.int32),
         ],
         cost_estimate=pl.CostEstimate(
             flops=16 * records.size, bytes_accessed=3 * records.size, transcendentals=0
         ),
         compiler_params=params(60),
         name="normal_terms",
-    )(window_start, window_stop, records)
+    )(tile_ranks, window_start, window_stop, records)
 
 
 def on_device(start_model, v_basis, u_basis, records, tile_ranks, window_start, window_stop):
@@ -416,13 +444,16 @@
         compiler_params=params(60),
         name="first_projection",
     )(tile_ranks, v_basis, start_model)
-    normal = normal_terms(phases, window_start, window_stop, records)
+    *normal, starts = normal_terms(
+        phases, pieces, tile_ranks, window_start, window_stop, records
+    )
     in_hbm = lambda x: pltpu.with_memory_space_constraint(x, pltpu.HBM)
     fetch = [
+        pltpu.SMEM(tile_ranks.shape, tile_ranks.dtype),
         pltpu.VMEM(slots.shape, BF16),
         *[pltpu.VMEM(x.shape, F32) for x in normal],
         pltpu.VMEM((freqs, 2 * lanes, receivers), F32),
-        pltpu.SemaphoreType.DMA((3,)),
+        pltpu.SemaphoreType.DMA((4,)),
     ]
     finish = [
         pltpu.VMEM(start_model.shape, F32),
@@ -435,7 +466,7 @@
         arrived = exchange(outgoing)
         outgoing = pl.pallas_call(
             functools.partial(misfit_kernel, pieces, cold),
-            in_specs=[SMEM, HBM, VMEM, HBM, HBM] if cold else [SMEM] + [VMEM] * 4,
+            in_specs=[HBM, HBM, VMEM, HBM, HBM] if cold else [VMEM] * 5,
             out_specs=VMEM,
             out_shape=slots,
             scratch_shapes=[
@@ -446,18 +477,18 @@
             + (fetch if cold else []),
             compiler_params=params(8 + mebibytes(slots, *normal)),
             name="misfit",
-        )(tile_ranks, arrived, u_basis, *terms)
+        )(tile_ranks if cold else starts, arrived, u_basis, *terms)
         arrived = exchange(outgoing)
         last = iteration == ITERS - 1
         result = pl.pallas_call(
             functools.partial(update_kernel, pieces, last),
-            in_specs=[SMEM] + [VMEM] * 3,
+            in_specs=[VMEM] * 4,
             out_specs=HBM if last else [VMEM, VMEM],
             out_shape=model if last else [model, slots],
             scratch_shapes=[padded_rows, left] + (finish if last else [waves]),
             compiler_params=params(12),
             name="last_update" if last else "update",
-        )(tile_ranks, arrived, v_basis, current)
+        )(starts, arrived, v_basis, current)
         if last:
             current = result
         else:

time: 118 us -> 116 us (0.983)
  Pallas kernels: 27.6 us -> 24.8 us
    pallas_call x2, Pallas kernels: 7.8 us -> 6.17 us  [on_device(): pl.pallas_call(functools.partial(misfit_kernel, pieces, cold), in_specs=[...]
    pallas_call x2, Pallas kernels: 5.8 us -> 4.46 us  [on_device(): pl.pallas_call(functools.partial(update_kernel, pieces, last), in_specs=[...]
  transfers between devices with their start and end apart: 1 -> 1, of which waited for: 1 -> 1; matrix products, arithmetic and copies ran while one was open for 0% -> 0% of each run, Pallas kernels for 8% -> 9%
where the time goes in v2:
time: 116 us; the launch traced here: 115 us
  blocking collectives  74 us (64%)
  Pallas kernels  24.8 us (21%)
  waiting for transfers between devices  8.82 us (8%)
  starting transfers between devices  7.36 us (6%)
    all_to_all x3, blocking collectives, on_device(): lax.all_to_all(x, 'tile', split_axis=0, concat_axis=0, tiled=True)  74 us
    pallas_call x1, Pallas kernels, normal_terms(): pl.pallas_call(functools.partial(normal_kernel, phases, pieces), grid=(wi...  9.82 us
    all_to_all x1, waiting for transfers between devices, on_device(): lax.all_to_all(x, 'tile', split_axis=0, concat_axis=0, tiled=True)  8.82 us
    all_to_all x1, starting transfers between devices, on_device(): lax.all_to_all(x, 'tile', split_axis=0, concat_axis=0, tiled=True)  7.36 us
    pallas_call x2, Pallas kernels, on_device(): pl.pallas_call(functools.partial(misfit_kernel, pieces, cold), in_specs=[...  6.17 us
    pallas_call x2, Pallas kernels, on_device(): pl.pallas_call(functools.partial(update_kernel, pieces, last), in_specs=[...  4.46 us
    pallas_call x1, Pallas kernels, on_device(): pl.pallas_call(functools.partial(first_kernel, pieces), in_specs=[HBM, HB...  4.33 us
  transfers between devices with their start and end apart: 1, of which 1 were waited for; matrix products, arithmetic and copies ran while one was open for 0% of the time, Pallas kernels for 9%

profile of v2, /device:TPU:1, one launch (start us, length us, event | category | flops | bytes accessed | tf_op | source)
XLA Modules:
  0.0 115.1 jit_solution(11721486659932760381)
XLA Ops:
  0.0 4.3 %first_projection.1 = bf16[16,96,256]{2,1,0:T(8,128)(2,1)} custom-call(s32[1,16,16]{2,1,0:T(8,128)} %starts_ref.1, bf16[2,832,1024]{2,1,0:T(8,128)(2,1)} %v_ref.3, f32[2,1024,128]{2,1,0:T(8,128)} %x_ref.1), custom_call_target="tpu_custom_call" | custom-call | tf_op jit(solution)/shard_map/first_projection/pallas_call | solution.py:429
  4.3 7.4 %all-to-all-start = ((bf16[16,96,256]{2,1,0:T(8,128)(2,1)}), bf16[16,96,256]{2,1,0:T(8,128)(2,1)}, u32[]{:S(2)}, u32[]{:S(2)}) async-start(bf16[16,96,256]{2,1,0:T(8,128)(2,1)} %first_projection.1), calls=%async_computation | async-start | bytes 1572864 | tf_op jit(solution)/shard_map/all_to_all | solution.py:427
  11.7 0.0 copy-start.1
  11.7 0.0 copy-start.6
  11.7 9.8 %normal_terms.1 = (f32[3,128,1024]{2,1,0:T(8,128)}, f32[2,128,1024]{2,1,0:T(8,128)}, s32[32,128]{1,0:T(8,128)}) custom-call(s32[1,16,16]{2,1,0:T(8,128)} %starts_ref.1, s32[128,1024]{1,0:T(8,128)} %start_ref.1, s32[128,1024]{1,0:T(8,128)} %stop_ref.1, bf16[32,128,1024]{2,1,0:T(8,128)(2,1)} %records_ref.1), custom_call_target="tpu_custom_call" | custom-call | flops 67108864 | bytes 12582912 | tf_op jit(solution)/shard_map/normal_terms/pallas_call | solution.py:386
  21.5 8.8 %all-to-all-done.in_ref = bf16[16,96,256]{2,1,0:T(8,128)(2,1)} async-done(((bf16[16,96,256]{2,1,0:T(8,128)(2,1)}), bf16[16,96,256]{2,1,0:T(8,128)(2,1)}, u32[]{:S(2)}, u32[]{:S(2)}) %all-to-all-start) | async-done | bytes 786464 | tf_op jit(solution)/shard_map/all_to_all | solution.py:427
  30.4 0.0 copy-done.1
  30.4 0.0 copy-done.6
  30.4 0.0 copy-start
  30.4 0.0 copy-start.5
  30.4 3.8 %misfit.2 = bf16[16,96,256]{2,1,0:T(8,128)(2,1)S(1)} custom-call(s32[1,16,16]{2,1,0:T(8,128)S(1)} %copy-done.6, bf16[16,96,256]{2,1,0:T(8,128)(2,1)} %all-to-all-done.in_ref, bf16[2,1,832,1024]{3,2,1,0:T(8,128)(2,1)S(1)} %copy-done.1, f32[3,128,1024]{2,1,0:T(8,128)} %get-tuple-element.11.gram_ref, f32[2,128,1024]{2,1,0:T(8,128)} %get-tuple-element.12.data_ref), custom_call_target="tpu_custom_call" | custom-call | tf_op jit(solution)/shard_map/misfit/pallas_call | solution.py:467
  34.2 26.1 %all_to_all.20.in_ref = bf16[16,96,256]{2,1,0:T(8,128)(2,1)S(1)} all-to-all(bf16[16,96,256]{2,1,0:T(8,128)(2,1)S(1)} %misfit.2), channel_id=1, replica_groups=mesh['groups'=2,'tile'=16] {'tile'}, dimensions={0} | all-to-all | bytes 1572864 | tf_op jit(solution)/shard_map/all_to_all | solution.py:427
  60.2 0.0 copy-done
  60.2 0.0 copy-done.3
  60.2 0.0 copy-done.5
  60.2 0.0 copy-start.2
  60.3 0.0 copy-start.4
  60.3 2.2 %update.1 = (f32[2,1024,128]{2,1,0:T(8,128)S(1)}, bf16[16,96,256]{2,1,0:T(8,128)(2,1)S(1)}) custom-call(s32[32,128]{1,0:T(8,128)S(1)} %copy-done.5, bf16[16,96,256]{2,1,0:T(8,128)(2,1)S(1)} %all_to_all.20.in_ref, bf16[2,832,1024]{2,1,0:T(8,128)(2,1)S(1)} %copy-done, f32[2,1024,128]{2,1,0:T(8,128)S(1)} %copy-done.3), custom_call_target="tpu_custom_call" | custom-call | tf_op jit(solution)/shard_map/update/pallas_call | solution.py:483
  62.5 24.0 %all_to_all.21.in_ref = bf16[16,96,256]{2,1,0:T(8,128)(2,1)S(1)} all-to-all(bf16[16,96,256]{2,1,0:T(8,128)(2,1)S(1)} %get-tuple-element.13), channel_id=1, replica_groups=mesh['groups'=2,'tile'=16] {'tile'}, dimensions={0} | all-to-all | bytes 1572864 | tf_op jit(solution)/shard_map/all_to_all | solution.py:427
  86.5 0.0 copy-done.2
  86.5 0.0 copy-done.4
  86.5 2.4 %misfit.3 = bf16[16,96,256]{2,1,0:T(8,128)(2,1)S(1)} custom-call(s32[32,128]{1,0:T(8,128)S(1)} %copy-done.5, bf16[16,96,256]{2,1,0:T(8,128)(2,1)S(1)} %all_to_all.21.in_ref, bf16[2,1,832,1024]{3,2,1,0:T(8,128)(2,1)S(1)} %copy-done.1, f32[3,128,1024]{2,1,0:T(8,128)S(1)} %copy-done.2, f32[2,128,1024]{2,1,0:T(8,128)S(1)} %copy-done.4), custom_call_target="tpu_custom_call" | custom-call | tf_op jit(solution)/shard_map/misfit/pallas_call | solution.py:467
  88.9 24.0 %all_to_all.22.in_ref = bf16[16,96,256]{2,1,0:T(8,128)(2,1)S(1)} all-to-all(bf16[16,96,256]{2,1,0:T(8,128)(2,1)S(1)} %misfit.3), channel_id=1, replica_groups=mesh['groups'=2,'tile'=16] {'tile'}, dimensions={0} | all-to-all | bytes 1572864 | tf_op jit(solution)/shard_map/all_to_all | solution.py:427
  112.9 2.2 %last_update.1 = f32[2,1024,128]{2,1,0:T(8,128)} custom-call(s32[32,128]{1,0:T(8,128)S(1)} %copy-done.5, bf16[16,96,256]{2,1,0:T(8,128)(2,1)S(1)} %all_to_all.22.in_ref, bf16[2,832,1024]{2,1,0:T(8,128)(2,1)S(1)} %copy-done, f32[2,1024,128]{2,1,0:T(8,128)S(1)} %get-tuple-element.14.x_ref), custom_call_target="tpu_custom_call" | custom-call | tf_op jit(solution)/shard_map/last_update/pallas_call | solution.py:483
  (1 shorter events, 0.0 us)
Async XLA Ops:
  4.3 26.0 %all-to-all-start = ((bf16[16,96,256]{2,1,0:T(8,128)(2,1)}), bf16[16,96,256]{2,1,0:T(8,128)(2,1)}, u32[]{:S(2)}, u32[]{:S(2)}) async-start(bf16[16,96,256]{2,1,0:T(8,128)(2,1)} %first_projection.1), calls=%async_computation | async-start | bytes 1572864 | tf_op jit(solution)/shard_map/all_to_all | solution.py:427
  11.7 18.7 %copy-start.1 = (bf16[2,1,832,1024]{3,2,1,0:T(8,128)(2,1)S(1)}, bf16[2,1,832,1024]{3,2,1,0:T(8,128)(2,1)}, u32[]{:S(2)}) copy-start(bf16[2,1,832,1024]{3,2,1,0:T(8,128)(2,1)} %u_ref.3) | copy-start | bytes 10223620
  11.7 18.7 %copy-start.6 = (s32[1,16,16]{2,1,0:T(8,128)S(1)}, s32[1,16,16]{2,1,0:T(8,128)}, u32[]{:S(2)}) copy-start(s32[1,16,16]{2,1,0:T(8,128)} %starts_ref.1) | copy-start | bytes 3076
  30.4 29.9 %copy-start = (bf16[2,832,1024]{2,1,0:T(8,128)(2,1)S(1)}, bf16[2,832,1024]{2,1,0:T(8,128)(2,1)}, u32[]{:S(2)}) copy-start(bf16[2,832,1024]{2,1,0:T(8,128)(2,1)} %v_ref.3) | copy-start | bytes 10223620
  30.4 29.9 %copy-start.3 = (f32[2,1024,128]{2,1,0:T(8,128)S(1)}, f32[2,1024,128]{2,1,0:T(8,128)}, u32[]{:S(2)}) copy-start(f32[2,1024,128]{2,1,0:T(8,128)} %x_ref.1) | copy-start | bytes 3145732
  30.4 29.9 %copy-start.5 = (s32[32,128]{1,0:T(8,128)S(1)}, s32[32,128]{1,0:T(8,128)}, u32[]{:S(2)}) copy-start(s32[32,128]{1,0:T(8,128)} %get-tuple-element.10.starts_ref) | copy-start | bytes 49156
  60.2 26.3 %copy-start.2 = (f32[3,128,1024]{2,1,0:T(8,128)S(1)}, f32[3,128,1024]{2,1,0:T(8,128)}, u32[]{:S(2)}) copy-start(f32[3,128,1024]{2,1,0:T(8,128)} %get-tuple-element.11.gram_ref) | copy-start | bytes 4718596
  60.3 26.3 %copy-start.4 = (f32[2,128,1024]{2,1,0:T(8,128)S(1)}, f32[2,128,1024]{2,1,0:T(8,128)}, u32[]{:S(2)}) copy-start(f32[2,128,1024]{2,1,0:T(8,128)} %get-tuple-element.12.data_ref) | copy-start | bytes 3145732

commit v3 on v2

--- a/solution.py
+++ b/solution.py
@@ -195,7 +195,7 @@
     cols = in_ref.shape[0] // freqs
     if cold:
         slots_hbm, gram_hbm, data_hbm = in_ref, gram_ref, data_ref
-        out_ref, rows_ref, left_ref, field_ref, *fetch = rest
+        v_hbm, x_hbm, out_ref, v_ref, x_ref, rows_ref, left_ref, field_ref, *fetch = rest
         ranks_hbm = starts_ref
         ranks_ref, in_ref, gram_ref, data_ref, pred_ref, sems = fetch
         pairs = [
@@ -203,6 +203,8 @@
             (slots_hbm, in_ref),
             (gram_hbm, gram_ref),
             (data_hbm, data_ref),
+            (v_hbm, v_ref),
+            (x_hbm, x_ref),
         ]
         copies = [pltpu.make_async_copy(*pair, sems.at[n]) for n, pair in enumerate(pairs)]
         for copy in copies:
@@ -248,6 +250,9 @@
         value = dot_last(u_ref[0, f], field_ref[f, 0]) + dot_last(u_ref[1, f], field_ref[f, 1])
         store_rows(rows_ref, rank_total, value)
         store_slots(starts[f], rows_ref, out_ref, 1, f * cols)
+    if cold:
+        copies[4].wait()
+        copies[5].wait()
 
 
 def update_kernel(pieces, last, starts_ref, in_ref, v_ref, x_ref, *rest):
@@ -421,6 +426,7 @@
 
     slots = jax.ShapeDtypeStruct((tiles, RMAX, 2 * lanes), BF16)
     model = jax.ShapeDtypeStruct(start_model.shape, F32)
+    v_like = jax.ShapeDtypeStruct(v_basis.shape, BF16)
     padded_rows = pltpu.VMEM((2, rank_total + RMAX, lanes), F32)
     waves = pltpu.VMEM((2, points, 2 * lanes), BF16)
     left = pltpu.VMEM((2 * lanes, 2 * rank_total), BF16)
@@ -453,7 +459,7 @@
         pltpu.VMEM(slots.shape, BF16),
         *[pltpu.VMEM(x.shape, F32) for x in normal],
         pltpu.VMEM((freqs, 2 * lanes, receivers), F32),
-        pltpu.SemaphoreType.DMA((4,)),
+        pltpu.SemaphoreType.DMA((6,)),
     ]
     finish = [
         pltpu.VMEM(start_model.shape, F32),
@@ -463,21 +469,26 @@
     for iteration in range(ITERS):
         cold = iteration == 0
         terms = [in_hbm(x) for x in normal] if cold else normal
+        early = [in_hbm(v_basis), in_hbm(current)] if cold else []
         arrived = exchange(outgoing)
-        outgoing = pl.pallas_call(
+        result = pl.pallas_call(
             functools.partial(misfit_kernel, pieces, cold),
-            in_specs=[HBM, HBM, VMEM, HBM, HBM] if cold else [VMEM] * 5,
-            out_specs=VMEM,
-            out_shape=slots,
+            in_specs=[HBM, HBM, VMEM, HBM, HBM, HBM, HBM] if cold else [VMEM] * 5,
+            out_specs=[VMEM] * 3 if cold else VMEM,
+            out_shape=[slots, v_like, model] if cold else slots,
             scratch_shapes=[
                 padded_rows,
                 pltpu.VMEM((freqs, 2 * lanes, 2 * rank_total), BF16),
                 pltpu.VMEM((freqs, 2, 2 * lanes, receivers), BF16),
             ]
             + (fetch if cold else []),
-            compiler_params=params(8 + mebibytes(slots, *normal)),
+            compiler_params=params(8 + mebibytes(slots, v_basis, model, *normal)),
             name="misfit",
-        )(tile_ranks if cold else starts, arrived, u_basis, *terms)
+        )(tile_ranks if cold else starts, arrived, u_basis, *terms, *early)
+        if cold:
+            outgoing, v_basis, current = result
+        else:
+            outgoing = result
         arrived = exchange(outgoing)
         last = iteration == ITERS - 1
         result = pl.pallas_call(

time: 116 us -> 115 us (level)
  no operation moved by 1% of the time
where the time goes in v3:
time: 115 us
  blocking collectives  74 us (64%)
  Pallas kernels  24.6 us (21%)
  waiting for transfers between devices  8.82 us (8%)
  starting transfers between devices  7.36 us (6%)
    all_to_all x3, blocking collectives, on_device(): lax.all_to_all(x, 'tile', split_axis=0, concat_axis=0, tiled=True)  74 us
    pallas_call x1, Pallas kernels, normal_terms(): pl.pallas_call(functools.partial(normal_kernel, phases, pieces), grid=(wi...  9.82 us
    all_to_all x1, waiting for transfers between devices, on_device(): lax.all_to_all(x, 'tile', split_axis=0, concat_axis=0, tiled=True)  8.82 us
    all_to_all x1, starting transfers between devices, on_device(): lax.all_to_all(x, 'tile', split_axis=0, concat_axis=0, tiled=True)  7.36 us
    pallas_call x2, Pallas kernels, on_device(): pl.pallas_call(functools.partial(misfit_kernel, pieces, cold), in_specs=[...  6.05 us
    pallas_call x2, Pallas kernels, on_device(): pl.pallas_call(functools.partial(update_kernel, pieces, last), in_specs=[...  4.46 us
    pallas_call x1, Pallas kernels, on_device(): pl.pallas_call(functools.partial(first_kernel, pieces), in_specs=[HBM, HB...  4.31 us
  transfers between devices with their start and end apart: 1, of which 1 were waited for; matrix products, arithmetic and copies ran while one was open for 0% of the time, Pallas kernels for 9%

profile of v3, /device:TPU:1, one launch (start us, length us, event | category | flops | bytes accessed | tf_op | source)
XLA Modules:
  0.0 114.9 jit_solution(939026111252178355)
XLA Ops:
  0.0 4.3 %first_projection.1 = bf16[16,96,256]{2,1,0:T(8,128)(2,1)} custom-call(s32[1,16,16]{2,1,0:T(8,128)} %starts_ref.1, bf16[2,832,1024]{2,1,0:T(8,128)(2,1)} %rest_0_.1, f32[2,1024,128]{2,1,0:T(8,128)} %rest_1_.1), custom_call_target="tpu_custom_call" | custom-call | tf_op jit(solution)/shard_map/first_projection/pallas_call | solution.py:435
  4.3 7.4 %all-to-all-start = ((bf16[16,96,256]{2,1,0:T(8,128)(2,1)}), bf16[16,96,256]{2,1,0:T(8,128)(2,1)}, u32[]{:S(2)}, u32[]{:S(2)}) async-start(bf16[16,96,256]{2,1,0:T(8,128)(2,1)} %first_projection.1), calls=%async_computation | async-start | bytes 1572864 | tf_op jit(solution)/shard_map/all_to_all | solution.py:433
  11.7 0.0 copy-start
  11.7 0.0 copy-start.4
  11.7 9.8 %normal_terms.1 = (f32[3,128,1024]{2,1,0:T(8,128)}, f32[2,128,1024]{2,1,0:T(8,128)}, s32[32,128]{1,0:T(8,128)}) custom-call(s32[1,16,16]{2,1,0:T(8,128)} %starts_ref.1, s32[128,1024]{1,0:T(8,128)} %start_ref.1, s32[128,1024]{1,0:T(8,128)} %stop_ref.1, bf16[32,128,1024]{2,1,0:T(8,128)(2,1)} %records_ref.1), custom_call_target="tpu_custom_call" | custom-call | flops 67108864 | bytes 12582912 | tf_op jit(solution)/shard_map/normal_terms/pallas_call | solution.py:391
  21.5 8.8 %all-to-all-done.in_ref = bf16[16,96,256]{2,1,0:T(8,128)(2,1)} async-done(((bf16[16,96,256]{2,1,0:T(8,128)(2,1)}), bf16[16,96,256]{2,1,0:T(8,128)(2,1)}, u32[]{:S(2)}, u32[]{:S(2)}) %all-to-all-start) | async-done | bytes 786464 | tf_op jit(solution)/shard_map/all_to_all | solution.py:433
  30.3 0.0 copy-done
  30.3 0.0 copy-done.4
  30.3 0.0 copy-start.3
  30.4 3.7 %misfit.2 = (bf16[16,96,256]{2,1,0:T(8,128)(2,1)S(1)}, bf16[2,832,1024]{2,1,0:T(8,128)(2,1)S(1)}, f32[2,1024,128]{2,1,0:T(8,128)S(1)}) custom-call(s32[1,16,16]{2,1,0:T(8,128)S(1)} %copy-done.4, bf16[16,96,256]{2,1,0:T(8,128)(2,1)} %all-to-all-done.in_ref, bf16[2,1,832,1024]{3,2,1,0:T(8,128)(2,1)S(1)} %copy-done, ...), custom_call_target="tpu_custom_call" | custom-call | tf_op jit(solution)/shard_map/misfit/pallas_call | solution.py:474
  34.0 26.1 %all_to_all.20.in_ref = bf16[16,96,256]{2,1,0:T(8,128)(2,1)S(1)} all-to-all(bf16[16,96,256]{2,1,0:T(8,128)(2,1)S(1)} %get-tuple-element.16), channel_id=1, replica_groups=mesh['groups'=2,'tile'=16] {'tile'}, dimensions={0} | all-to-all | bytes 1572864 | tf_op jit(solution)/shard_map/all_to_all | solution.py:433
  60.1 0.0 copy-done.3
  60.1 0.0 copy-start.1
  60.1 0.0 copy-start.2
  60.1 2.3 %update.1 = (f32[2,1024,128]{2,1,0:T(8,128)S(1)}, bf16[16,96,256]{2,1,0:T(8,128)(2,1)S(1)}) custom-call(s32[32,128]{1,0:T(8,128)S(1)} %copy-done.3, bf16[16,96,256]{2,1,0:T(8,128)(2,1)S(1)} %all_to_all.20.in_ref, bf16[2,832,1024]{2,1,0:T(8,128)(2,1)S(1)} %get-tuple-element.17.v_ref, f32[2,1024,128]{2,1,0:T(8,128)S(1)} %get-tuple-element.18.x_ref), custom_call_target="tpu_custom_call" | custom-call | tf_op jit(solution)/shard_map/update/pallas_call | solution.py:494
  62.4 24.0 %all_to_all.21.in_ref = bf16[16,96,256]{2,1,0:T(8,128)(2,1)S(1)} all-to-all(bf16[16,96,256]{2,1,0:T(8,128)(2,1)S(1)} %get-tuple-element.19), channel_id=1, replica_groups=mesh['groups'=2,'tile'=16] {'tile'}, dimensions={0} | all-to-all | bytes 1572864 | tf_op jit(solution)/shard_map/all_to_all | solution.py:433
  86.3 0.0 copy-done.1
  86.3 0.0 copy-done.2
  86.3 2.4 %misfit.3 = bf16[16,96,256]{2,1,0:T(8,128)(2,1)S(1)} custom-call(s32[32,128]{1,0:T(8,128)S(1)} %copy-done.3, bf16[16,96,256]{2,1,0:T(8,128)(2,1)S(1)} %all_to_all.21.in_ref, bf16[2,1,832,1024]{3,2,1,0:T(8,128)(2,1)S(1)} %copy-done, f32[3,128,1024]{2,1,0:T(8,128)S(1)} %copy-done.1, f32[2,128,1024]{2,1,0:T(8,128)S(1)} %copy-done.2), custom_call_target="tpu_custom_call" | custom-call | tf_op jit(solution)/shard_map/misfit/pallas_call | solution.py:474
  88.7 24.0 %all_to_all.22.in_ref = bf16[16,96,256]{2,1,0:T(8,128)(2,1)S(1)} all-to-all(bf16[16,96,256]{2,1,0:T(8,128)(2,1)S(1)} %misfit.3), channel_id=1, replica_groups=mesh['groups'=2,'tile'=16] {'tile'}, dimensions={0} | all-to-all | bytes 1572864 | tf_op jit(solution)/shard_map/all_to_all | solution.py:433
  112.7 2.2 %last_update.1 = f32[2,1024,128]{2,1,0:T(8,128)} custom-call(s32[32,128]{1,0:T(8,128)S(1)} %copy-done.3, bf16[16,96,256]{2,1,0:T(8,128)(2,1)S(1)} %all_to_all.22.in_ref, bf16[2,832,1024]{2,1,0:T(8,128)(2,1)S(1)} %get-tuple-element.17.v_ref, f32[2,1024,128]{2,1,0:T(8,128)S(1)} %get-tuple-element.20.x_ref), custom_call_target="tpu_custom_call" | custom-call | tf_op jit(solution)/shard_map/last_update/pallas_call | solution.py:494
Async XLA Ops:
  4.3 26.0 %all-to-all-start = ((bf16[16,96,256]{2,1,0:T(8,128)(2,1)}), bf16[16,96,256]{2,1,0:T(8,128)(2,1)}, u32[]{:S(2)}, u32[]{:S(2)}) async-start(bf16[16,96,256]{2,1,0:T(8,128)(2,1)} %first_projection.1), calls=%async_computation | async-start | bytes 1572864 | tf_op jit(solution)/shard_map/all_to_all | solution.py:433
  11.7 18.7 %copy-start = (bf16[2,1,832,1024]{3,2,1,0:T(8,128)(2,1)S(1)}, bf16[2,1,832,1024]{3,2,1,0:T(8,128)(2,1)}, u32[]{:S(2)}) copy-start(bf16[2,1,832,1024]{3,2,1,0:T(8,128)(2,1)} %u_ref.3) | copy-start | bytes 10223620
  11.7 18.7 %copy-start.4 = (s32[1,16,16]{2,1,0:T(8,128)S(1)}, s32[1,16,16]{2,1,0:T(8,128)}, u32[]{:S(2)}) copy-start(s32[1,16,16]{2,1,0:T(8,128)} %starts_ref.1) | copy-start | bytes 3076
  30.3 29.7 %copy-start.3 = (s32[32,128]{1,0:T(8,128)S(1)}, s32[32,128]{1,0:T(8,128)}, u32[]{:S(2)}) copy-start(s32[32,128]{1,0:T(8,128)} %get-tuple-element.13.starts_ref) | copy-start | bytes 49156
  60.1 26.2 %copy-start.1 = (f32[3,128,1024]{2,1,0:T(8,128)S(1)}, f32[3,128,1024]{2,1,0:T(8,128)}, u32[]{:S(2)}) copy-start(f32[3,128,1024]{2,1,0:T(8,128)} %get-tuple-element.14.gram_ref) | copy-start | bytes 4718596
  60.1 26.2 %copy-start.2 = (f32[2,128,1024]{2,1,0:T(8,128)S(1)}, f32[2,128,1024]{2,1,0:T(8,128)}, u32[]{:S(2)}) copy-start(f32[2,128,1024]{2,1,0:T(8,128)} %get-tuple-element.15.data_ref) | copy-start | bytes 3145732

commit v4 on v3

--- a/solution.py
+++ b/solution.py
@@ -207,10 +207,12 @@
             (x_hbm, x_ref),
         ]
         copies = [pltpu.make_async_copy(*pair, sems.at[n]) for n, pair in enumerate(pairs)]
-        for copy in copies:
+        for copy in copies[:4]:
             copy.start()
         copies[0].wait()
         copies[1].wait()
+        for copy in copies[4:]:
+            copy.start()
         starts = row_starts(ranks_ref, pieces)
     else:
         out_ref, rows_ref, left_ref, field_ref = rest

time: 115 us -> 115 us (level)
  no operation moved by 1% of the time
where the time goes in v4:
time: 115 us
  blocking collectives  74 us (64%)
  Pallas kernels  24.6 us (21%)
  waiting for transfers between devices  8.82 us (8%)
  starting transfers between devices  7.36 us (6%)
    all_to_all x3, blocking collectives, on_device(): lax.all_to_all(x, 'tile', split_axis=0, concat_axis=0, tiled=True)  74 us
    pallas_call x1, Pallas kernels, normal_terms(): pl.pallas_call(functools.partial(normal_kernel, phases, pieces), grid=(wi...  9.82 us
    all_to_all x1, waiting for transfers between devices, on_device(): lax.all_to_all(x, 'tile', split_axis=0, concat_axis=0, tiled=True)  8.82 us
    all_to_all x1, starting transfers between devices, on_device(): lax.all_to_all(x, 'tile', split_axis=0, concat_axis=0, tiled=True)  7.36 us
    pallas_call x2, Pallas kernels, on_device(): pl.pallas_call(functools.partial(misfit_kernel, pieces, cold), in_specs=[...  6.06 us
    pallas_call x2, Pallas kernels, on_device(): pl.pallas_call(functools.partial(update_kernel, pieces, last), in_specs=[...  4.45 us
    pallas_call x1, Pallas kernels, on_device(): pl.pallas_call(functools.partial(first_kernel, pieces), in_specs=[HBM, HB...  4.31 us
  transfers between devices with their start and end apart: 1, of which 1 were waited for; matrix products, arithmetic and copies ran while one was open for 0% of the time, Pallas kernels for 9%

profile of v4, /device:TPU:1, one launch (start us, length us, event | category | flops | bytes accessed | tf_op | source)
XLA Modules:
  0.0 114.9 jit_solution(17385020592864620715)
XLA Ops:
  0.0 4.3 %first_projection.1 = bf16[16,96,256]{2,1,0:T(8,128)(2,1)} custom-call(s32[1,16,16]{2,1,0:T(8,128)} %starts_ref.1, bf16[2,832,1024]{2,1,0:T(8,128)(2,1)} %rest_0_.1, f32[2,1024,128]{2,1,0:T(8,128)} %rest_1_.1), custom_call_target="tpu_custom_call" | custom-call | tf_op jit(solution)/shard_map/first_projection/pallas_call | solution.py:437
  4.3 7.4 %all-to-all-start = ((bf16[16,96,256]{2,1,0:T(8,128)(2,1)}), bf16[16,96,256]{2,1,0:T(8,128)(2,1)}, u32[]{:S(2)}, u32[]{:S(2)}) async-start(bf16[16,96,256]{2,1,0:T(8,128)(2,1)} %first_projection.1), calls=%async_computation | async-start | bytes 1572864 | tf_op jit(solution)/shard_map/all_to_all | solution.py:435
  11.7 0.0 copy-start
  11.7 0.0 copy-start.4
  11.7 9.8 %normal_terms.1 = (f32[3,128,1024]{2,1,0:T(8,128)}, f32[2,128,1024]{2,1,0:T(8,128)}, s32[32,128]{1,0:T(8,128)}) custom-call(s32[1,16,16]{2,1,0:T(8,128)} %starts_ref.1, s32[128,1024]{1,0:T(8,128)} %start_ref.1, s32[128,1024]{1,0:T(8,128)} %stop_ref.1, bf16[32,128,1024]{2,1,0:T(8,128)(2,1)} %records_ref.1), custom_call_target="tpu_custom_call" | custom-call | flops 67108864 | bytes 12582912 | tf_op jit(solution)/shard_map/normal_terms/pallas_call | solution.py:393
  21.5 8.8 %all-to-all-done.in_ref = bf16[16,96,256]{2,1,0:T(8,128)(2,1)} async-done(((bf16[16,96,256]{2,1,0:T(8,128)(2,1)}), bf16[16,96,256]{2,1,0:T(8,128)(2,1)}, u32[]{:S(2)}, u32[]{:S(2)}) %all-to-all-start) | async-done | bytes 786464 | tf_op jit(solution)/shard_map/all_to_all | solution.py:435
  30.3 0.0 copy-done
  30.3 0.0 copy-done.4
  30.3 0.0 copy-start.3
  30.4 3.7 %misfit.2 = (bf16[16,96,256]{2,1,0:T(8,128)(2,1)S(1)}, bf16[2,832,1024]{2,1,0:T(8,128)(2,1)S(1)}, f32[2,1024,128]{2,1,0:T(8,128)S(1)}) custom-call(s32[1,16,16]{2,1,0:T(8,128)S(1)} %copy-done.4, bf16[16,96,256]{2,1,0:T(8,128)(2,1)} %all-to-all-done.in_ref, bf16[2,1,832,1024]{3,2,1,0:T(8,128)(2,1)S(1)} %copy-done, ...), custom_call_target="tpu_custom_call" | custom-call | tf_op jit(solution)/shard_map/misfit/pallas_call | solution.py:476
  34.0 26.1 %all_to_all.20.in_ref = bf16[16,96,256]{2,1,0:T(8,128)(2,1)S(1)} all-to-all(bf16[16,96,256]{2,1,0:T(8,128)(2,1)S(1)} %get-tuple-element.16), channel_id=1, replica_groups=mesh['groups'=2,'tile'=16] {'tile'}, dimensions={0} | all-to-all | bytes 1572864 | tf_op jit(solution)/shard_map/all_to_all | solution.py:435
  60.1 0.0 copy-done.3
  60.1 0.0 copy-start.1
  60.1 0.0 copy-start.2
  60.1 2.2 %update.1 = (f32[2,1024,128]{2,1,0:T(8,128)S(1)}, bf16[16,96,256]{2,1,0:T(8,128)(2,1)S(1)}) custom-call(s32[32,128]{1,0:T(8,128)S(1)} %copy-done.3, bf16[16,96,256]{2,1,0:T(8,128)(2,1)S(1)} %all_to_all.20.in_ref, bf16[2,832,1024]{2,1,0:T(8,128)(2,1)S(1)} %get-tuple-element.17.v_ref, f32[2,1024,128]{2,1,0:T(8,128)S(1)} %get-tuple-element.18.x_ref), custom_call_target="tpu_custom_call" | custom-call | tf_op jit(solution)/shard_map/update/pallas_call | solution.py:496
  62.3 24.0 %all_to_all.21.in_ref = bf16[16,96,256]{2,1,0:T(8,128)(2,1)S(1)} all-to-all(bf16[16,96,256]{2,1,0:T(8,128)(2,1)S(1)} %get-tuple-element.19), channel_id=1, replica_groups=mesh['groups'=2,'tile'=16] {'tile'}, dimensions={0} | all-to-all | bytes 1572864 | tf_op jit(solution)/shard_map/all_to_all | solution.py:435
  86.3 0.0 copy-done.1
  86.3 0.0 copy-done.2
  86.3 2.4 %misfit.3 = bf16[16,96,256]{2,1,0:T(8,128)(2,1)S(1)} custom-call(s32[32,128]{1,0:T(8,128)S(1)} %copy-done.3, bf16[16,96,256]{2,1,0:T(8,128)(2,1)S(1)} %all_to_all.21.in_ref, bf16[2,1,832,1024]{3,2,1,0:T(8,128)(2,1)S(1)} %copy-done, f32[3,128,1024]{2,1,0:T(8,128)S(1)} %copy-done.1, f32[2,128,1024]{2,1,0:T(8,128)S(1)} %copy-done.2), custom_call_target="tpu_custom_call" | custom-call | tf_op jit(solution)/shard_map/misfit/pallas_call | solution.py:476
  88.7 24.0 %all_to_all.22.in_ref = bf16[16,96,256]{2,1,0:T(8,128)(2,1)S(1)} all-to-all(bf16[16,96,256]{2,1,0:T(8,128)(2,1)S(1)} %misfit.3), channel_id=1, replica_groups=mesh['groups'=2,'tile'=16] {'tile'}, dimensions={0} | all-to-all | bytes 1572864 | tf_op jit(solution)/shard_map/all_to_all | solution.py:435
  112.7 2.2 %last_update.1 = f32[2,1024,128]{2,1,0:T(8,128)} custom-call(s32[32,128]{1,0:T(8,128)S(1)} %copy-done.3, bf16[16,96,256]{2,1,0:T(8,128)(2,1)S(1)} %all_to_all.22.in_ref, bf16[2,832,1024]{2,1,0:T(8,128)(2,1)S(1)} %get-tuple-element.17.v_ref, f32[2,1024,128]{2,1,0:T(8,128)S(1)} %get-tuple-element.20.x_ref), custom_call_target="tpu_custom_call" | custom-call | tf_op jit(solution)/shard_map/last_update/pallas_call | solution.py:496
Async XLA Ops:
  4.3 26.0 %all-to-all-start = ((bf16[16,96,256]{2,1,0:T(8,128)(2,1)}), bf16[16,96,256]{2,1,0:T(8,128)(2,1)}, u32[]{:S(2)}, u32[]{:S(2)}) async-start(bf16[16,96,256]{2,1,0:T(8,128)(2,1)} %first_projection.1), calls=%async_computation | async-start | bytes 1572864 | tf_op jit(solution)/shard_map/all_to_all | solution.py:435
  11.7 18.7 %copy-start = (bf16[2,1,832,1024]{3,2,1,0:T(8,128)(2,1)S(1)}, bf16[2,1,832,1024]{3,2,1,0:T(8,128)(2,1)}, u32[]{:S(2)}) copy-start(bf16[2,1,832,1024]{3,2,1,0:T(8,128)(2,1)} %u_ref.3) | copy-start | bytes 10223620
  11.7 18.7 %copy-start.4 = (s32[1,16,16]{2,1,0:T(8,128)S(1)}, s32[1,16,16]{2,1,0:T(8,128)}, u32[]{:S(2)}) copy-start(s32[1,16,16]{2,1,0:T(8,128)} %starts_ref.1) | copy-start | bytes 3076
  30.3 29.7 %copy-start.3 = (s32[32,128]{1,0:T(8,128)S(1)}, s32[32,128]{1,0:T(8,128)}, u32[]{:S(2)}) copy-start(s32[32,128]{1,0:T(8,128)} %get-tuple-element.13.starts_ref) | copy-start | bytes 49156
  60.1 26.2 %copy-start.1 = (f32[3,128,1024]{2,1,0:T(8,128)S(1)}, f32[3,128,1024]{2,1,0:T(8,128)}, u32[]{:S(2)}) copy-start(f32[3,128,1024]{2,1,0:T(8,128)} %get-tuple-element.14.gram_ref) | copy-start | bytes 4718596
  60.1 26.2 %copy-start.2 = (f32[2,128,1024]{2,1,0:T(8,128)S(1)}, f32[2,128,1024]{2,1,0:T(8,128)}, u32[]{:S(2)}) copy-start(f32[2,128,1024]{2,1,0:T(8,128)} %get-tuple-element.15.data_ref) | copy-start | bytes 3145732
